TPU v7x, 128 devices: a whole 4x4x4 slice. The times are simulated.
128 devices in a mesh: kv: 32 (over x, y, core), head: 4 (over z).
Axes of the slice: x: 4, y: 4, z: 4, core: 2. Of those that a mesh axis runs over, the one named last changes fastest.
Arguments:
- queries: bfloat16 [16, 128, 128], P(None, 'head'), may hold values from -200 to 200
- k_cache: bfloat16 [16, 2048, 8, 128], P(None, 'kv', 'head'), may hold values from -6 to 6
- v_cache: bfloat16 [16, 2048, 8, 128], P(None, 'kv', 'head'), may hold values from -6 to 6
- lengths: int32 [16], replicated, may hold values from 1 to 2048, 17408 in all
- residual_in: bfloat16 [16, 16384], replicated, may hold values from -60 to 60
- out_weight: bfloat16 [16384, 16384], P(('head', 'kv')), may hold values from -2 to 2
- norm_gain: bfloat16 [16384], replicated, may hold values from 0.099609375 to 1.8984375
- gate_weight: bfloat16 [26624, 16384], P(('kv', 'head')), may hold values from -0.046875 to 0.046875
- up_weight: bfloat16 [26624, 16384], P(('kv', 'head')), may hold values from -0.046875 to 0.046875
- down_weight: bfloat16 [26624, 16384], P(('kv', 'head')), may hold values from -0.125 to 0.125
Outputs:
- mixed: bfloat16 [16, 16384], P(None, ('kv', 'head'))
All inputs are finite; a program needn't handle non-finite values.
Results may differ from a plain program's by a relative error of at most 0.015.
Values may be sent and summed in bfloat16 or wider, within the bound.
No kernel may reach another device: no remote copies, remote signals or barrier semaphores. Data moves between devices by JAX's collectives and lax.ppermute only.
A program may use at most 128 MiB of HBM per device.

v0:
```python
import jax
import jax.numpy as jnp
from jax import lax
from jax.sharding import PartitionSpec as P


def block_term(left, matrix, share_width, count):
    product = jnp.dot(left, matrix, preferred_element_type=jnp.float32)
    return product.reshape(left.shape[0], count, share_width).transpose(1, 0, 2)


def per_device(
    queries,
    k_cache,
    v_cache,
    lengths,
    residual_in,
    out_weight,
    norm_gain,
    gate_weight,
    up_weight,
    down_weight,
):
    batch_rows, local_heads, head_width = queries.shape
    span = k_cache.shape[1]
    local_groups = k_cache.shape[2]
    group_size = local_heads // local_groups
    shard_index = lax.axis_index("kv")
    positions = shard_index * span + jnp.arange(span, dtype=jnp.int32)
    live_slots = (positions[None, :] < lengths[:, None])[:, None, None, :]
    query_groups = queries.reshape(batch_rows, local_groups, group_size, head_width)
    scores = jnp.einsum(
        "bkgd,bskd->bkgs", query_groups, k_cache, preferred_element_type=jnp.float32
    ) * head_width ** (-0.5)
    masked = jnp.where(live_slots, scores, -1e30)
    block_max = jnp.max(masked, axis=-1)
    weights = jnp.where(live_slots, jnp.exp(masked - block_max[..., None]), 0.0)
    block_total = jnp.sum(weights, axis=-1)
    block_out = jnp.einsum(
        "bkgs,bskd->bkgd", weights.astype(jnp.bfloat16), v_cache, preferred_element_type=jnp.float32
    )
    block_max = block_max.reshape(batch_rows, local_heads)
    block_total = block_total.reshape(batch_rows, local_heads)
    block_out = block_out.reshape(batch_rows, local_heads, head_width)
    came_max, came_total, came_out = (
        lax.all_to_all(
            block_max[None].astype(jnp.bfloat16), "kv", split_axis=2, concat_axis=0, tiled=True
        ).astype(jnp.float32),
        lax.all_to_all(
            block_total[None].astype(jnp.bfloat16), "kv", split_axis=2, concat_axis=0, tiled=True
        ).astype(jnp.float32),
        lax.all_to_all(
            block_out[None].astype(jnp.bfloat16), "kv", split_axis=2, concat_axis=0, tiled=True
        ).astype(jnp.float32),
    )
    highest = jnp.max(came_max, axis=0)
    scales = jnp.exp(came_max - highest[None])
    merged_total = jnp.sum(scales * came_total, axis=0)
    merged_out = jnp.sum(scales[..., None] * came_out, axis=0)
    attended = (merged_out / merged_total[..., None]).reshape(batch_rows, -1).astype(jnp.bfloat16)
    width = residual_in.shape[1]
    devices = lax.axis_size(("kv", "head"))
    share_width = width // devices
    flat_index = lax.axis_index(("kv", "head"))
    projected = jnp.dot(attended, out_weight, preferred_element_type=jnp.float32)
    stream = residual_in.astype(jnp.float32) + lax.psum(projected, ("kv", "head"))
    factor = lax.rsqrt(jnp.mean(stream * stream, axis=1, keepdims=True) + 1e-05)
    normed = (stream * factor * norm_gain.astype(jnp.float32)).astype(jnp.bfloat16)
    stream_share = lax.dynamic_slice_in_dim(stream, flat_index * share_width, share_width, 1)
    gate = jnp.einsum("bd,fd->bf", normed, gate_weight, preferred_element_type=jnp.float32)
    upward = jnp.einsum("bd,fd->bf", normed, up_weight, preferred_element_type=jnp.float32)
    hidden = (jax.nn.silu(gate) * upward).astype(jnp.bfloat16)
    down_share = lax.psum_scatter(
        block_term(hidden, down_weight, share_width, lax.axis_size(("kv", "head")) * 1),
        ("kv", "head"),
        scatter_dimension=0,
        tiled=True,
    )
    return (stream_share + down_share[0]).astype(jnp.bfloat16)


def solution(mesh):
    placed = (
        P(None, "head", None),
        P(None, "kv", "head", None),
        P(None, "kv", "head", None),
        P(),
        P(),
        P(("head", "kv"), None),
        P(),
        P(("kv", "head"), None),
        P(("kv", "head"), None),
        P(("kv", "head"), None),
    )
    return jax.shard_map(
        per_device, mesh=mesh, in_specs=placed, out_specs=P(None, ("kv", "head")), check_vma=False
    )
```

profile of v0, /device:TPU:0, one launch (start us, length us, event | category | flops | bytes accessed | tf_op | source)
XLA Modules:
  0.0 859.1 jit_solution(13020994808264273557)
XLA Ops:
  6.5 0.0 copy-start
  6.5 0.8 broadcast_compare_fusion
  7.4 1.6 fusion.26
  9.0 0.1 convert_element_type.137
  9.1 0.7 copy.23
  9.8 7.4 all-to-all-start
  17.2 0.0 copy-done
  17.2 0.3 convolution_convert_fusion
  17.5 0.3 fusion.5
  17.8 0.1 convert_element_type.152
  17.9 0.7 copy.25
  18.6 0.7 copy.26
  19.3 5.2 all-to-all-done
  24.5 3.8 all-to-all-start.2
  28.4 0.1 fusion.25
  28.4 7.3 all-to-all-done.2
  35.7 3.9 all-to-all-start.1
  39.6 0.0 all-reduce.2.cloned.1.call-start
  39.7 7.8 all-to-all-done.1
  47.4 0.1 fusion.4
  47.6 3.9 fusion.20
  51.5 0.0 all-reduce.2.cloned.1.call-update
  51.6 0.0 reduce-scatter.2.cloned.1.call-start
  51.6 0.0 copy-done.2
  51.6 145.5 %all-reduce.2.cloned.1.call-done = f32[16,16384]{1,0:T(8,128)} async-done(((f32[16,16384]{1,0:T(8,128)}), f32[16,16384]{1,0:T(8,128)}) %all-reduce.2.cloned.1.call-update) | async-done | bytes 1048592 | tf_op jit(solution)/shard_map/psum | solution.py:66
  197.1 1.5 multiply_reduce_fusion
  198.6 4.8 fusion.24
  203.4 9.5 %convolution_bitcast_fusion = f32[2,128,8,128]{3,2,1,0:T(8,128)S(1)} fusion(bf16[208,16384]{1,0:T(8,128)(2,1)} %param.19, bf16[208,16384]{1,0:T(8,128)(2,1)} %param.18, f32[16,208]{1,0:T(8,128)S(1)} %fusion.24, f32[16,16384]{1,0:T(8,128)S(1)} %get-tuple-element.6, f32[16384]{0:T(1024)S(1)} %convert_element_type.158, f32[16]{0:T(128)S(1)} %add_rsqrt_fusion), kind=kOutput, calls=%fused_computation | convolution fusion | flops 218910208 | bytes 15807552 | tf_op jit(solution)/shard_map/dot_general | solution.py:8
  212.9 1.1 copy.38
  214.0 0.0 reduce-scatter.2.cloned.1.call-update
  214.1 636.9 %reduce-scatter.2.cloned.1.call-done = f32[1,16,128]{2,1,0:T(8,128)} async-done(((f32[128,16,128]{2,1,0:T(8,128)}), f32[1,16,128]{2,1,0:T(8,128)}) %reduce-scatter.2.cloned.1.call-update) | async-done | bytes 8208 | tf_op jit(solution)/shard_map/reduce_scatter | solution.py:73
  850.9 1.3 fusion.18
  (10 shorter events, 0.1 us)
Async XLA Ops:
  6.5 10.6 %copy-start = (bf16[16,64,2,128]{3,2,1,0:T(2,128)(2,1)S(1)}, bf16[16,64,2,128]{3,2,1,0:T(2,128)(2,1)}, u32[]{:S(2)}) copy-start(bf16[16,64,2,128]{3,2,1,0:T(2,128)(2,1)} %param.12) | copy-start | bytes 1572868
  6.5 45.1 %copy-start.2 = (bf16[16384]{0:T(1024)(128)(2,1)S(1)}, bf16[16384]{0:T(1024)(128)(2,1)}, u32[]{:S(2)}) copy-start(bf16[16384]{0:T(1024)(128)(2,1)} %param.16) | copy-start | bytes 98308
  6.5 190.6 %copy-start.1 = (bf16[16,16384]{1,0:T(8,128)(2,1)S(1)}, bf16[16,16384]{1,0:T(8,128)(2,1)}, u32[]{:S(2)}) copy-start(bf16[16,16384]{1,0:T(8,128)(2,1)} %param.14) | copy-start | bytes 1572868
  9.8 14.8 %all-to-all-start = ((bf16[1,16,32]{1,0,2:T(2,128)(2,1)}), bf16[1,16,32]{1,0,2:T(2,128)(2,1)S(1)}, u32[]{:S(2)}, u32[]{:S(2)}) async-start(bf16[1,16,32]{1,0,2:T(2,128)(2,1)} %copy.23), calls=%async_computation | async-start | bytes 32768 | tf_op jit(solution)/shard_map/all_to_all | solution.py:46
  24.5 11.2 %all-to-all-start.2 = ((bf16[1,16,32]{1,0,2:T(2,128)(2,1)}), bf16[1,16,32]{1,0,2:T(2,128)(2,1)S(1)}, u32[]{:S(2)}, u32[]{:S(2)}) async-start(bf16[1,16,32]{1,0,2:T(2,128)(2,1)} %copy.26), calls=%async_computation.2 | async-start | bytes 32768 | tf_op jit(solution)/shard_map/all_to_all | solution.py:49
  35.7 11.7 %all-to-all-start.1 = ((bf16[1,16,32,128]{3,1,0,2:T(8,128)(2,1)}), bf16[1,16,32,128]{3,1,0,2:T(8,128)(2,1)S(1)}, u32[]{:S(2)}, u32[]{:S(2)}) async-start(bf16[1,16,32,128]{3,1,0,2:T(8,128)(2,1)} %copy.25), calls=%async_computation.1 | async-start | bytes 262144 | tf_op jit(solution)/shard_map/all_to_all | solution.py:52
  39.6 157.6 %all-reduce.2.cloned.1.call-start = ((), (), s32[]{:S(2)}) async-start(), calls=%async_computation.4 | async-start | bytes 2097152 | tf_op jit(solution)/shard_map/psum | solution.py:66
  51.6 799.4 %reduce-scatter.2.cloned.1.call-start = ((), (), s32[]{:S(2)}) async-start(), calls=%async_computation.5 | async-start | bytes 1056768 | tf_op jit(solution)/shard_map/reduce_scatter | solution.py:73
Sparse Core Ops, SparseCore 0:
  51.7 145.4 all-reduce.1
  214.2 636.7 reduce-scatter.1
where the time goes:
time: 860 us; the launch traced here: 859 us
  waiting for transfers between devices  803 us (93%)
  matrix products  20.2 us (2%)
  starting transfers between devices  15.2 us (2%)
  between operations  13.5 us (2%)
    reduce_scatter x1, waiting for transfers between devices, per_device(): lax.psum_scatter(block_term(hidden, down_weight, share_width, lax.axis_si...  637 us
    psum x1, waiting for transfers between devices, per_device(): lax.psum(projected, ('kv', 'head'))  146 us
  transfers between devices with their start and end apart: 5, of which 5 were waited for; matrix products, arithmetic and copies ran while one was open for 0% of the time, Pallas kernels for 0%

commit v1 on v0

v1 whole, which is shorter than its diff:
```python
import jax
import jax.numpy as jnp
from jax import lax
from jax.sharding import Mesh, PartitionSpec as P

XY = ("x", "y")
KV = ("x", "y", "c")
ALL = ("x", "y", "c", "z")


def attention_message(queries, k_cache, v_cache, lengths):
    rows, heads, width = queries.shape
    span, groups = k_cache.shape[1], k_cache.shape[2]
    size = heads // groups
    positions = lax.axis_index(KV) * span + jnp.arange(span, dtype=jnp.int32)
    live = (positions[None, :] < lengths[:, None])[:, None, None, :]
    grouped = queries.reshape(rows, groups, size, width)
    scores = jnp.einsum(
        "bkgd,bskd->bkgs", grouped, k_cache, preferred_element_type=jnp.float32
    ) * width ** (-0.5)
    masked = jnp.where(live, scores, -1e30)
    point = jnp.max(masked, axis=-1).astype(jnp.bfloat16)
    weights = jnp.where(live, jnp.exp(masked - point.astype(jnp.float32)[..., None]), 0.0)
    total = jnp.sum(weights, axis=-1)
    out = jnp.einsum(
        "bkgs,bskd->bkgd", weights.astype(jnp.bfloat16), v_cache, preferred_element_type=jnp.float32
    )
    out = out.reshape(rows, heads, width).astype(jnp.bfloat16)
    stats = jnp.concatenate(
        [
            jnp.broadcast_to(a.reshape(rows, heads, 1).astype(jnp.bfloat16), (rows, heads, width // 2))
            for a in (point, total)
        ],
        axis=2,
    )
    return jnp.concatenate([out, stats], axis=0).transpose(1, 0, 2)


def merge(came, rows):
    out = came[:, :rows].astype(jnp.float32)
    width = out.shape[2]
    point = came[:, rows:, :1].astype(jnp.float32)
    total = came[:, rows:, width // 2 : width // 2 + 1].astype(jnp.float32)
    scale = jnp.exp(point - jnp.max(point, axis=0, keepdims=True))
    return jnp.sum(scale * out, axis=0) / jnp.sum(scale * total, axis=0)


def exchange(block, axis, flip):
    size = lax.axis_size(axis)
    return lax.ppermute(block, axis, [(i, i ^ flip) for i in range(size)])


def per_device(
    queries, k_cache, v_cache, lengths, residual_in, out_weight, norm_gain, gate_weight, up_weight, down_weight
):
    rows = queries.shape[0]
    width = residual_in.shape[1]
    message = attention_message(queries, k_cache, v_cache, lengths)
    came = lax.all_to_all(message, KV, split_axis=0, concat_axis=0, tiled=True)
    attended = merge(came, rows).astype(jnp.bfloat16)
    planes = lax.axis_size(XY)
    chunk = width // planes
    projected = jnp.dot(attended, out_weight, preferred_element_type=jnp.float32)
    pieces = projected.astype(jnp.bfloat16).reshape(rows, planes, chunk).transpose(1, 0, 2)
    pieces = lax.all_to_all(pieces, XY, split_axis=0, concat_axis=0, tiled=True)
    part = jnp.sum(pieces.astype(jnp.float32), axis=0)
    part = part + exchange(part, "c", 1)
    part = part + exchange(part, "z", 1)
    part = part + exchange(part, "z", 3)
    plane = lax.axis_index(XY)
    stream = part + lax.dynamic_slice_in_dim(residual_in, plane * chunk, chunk, 1).astype(jnp.float32)
    sent = jnp.broadcast_to(stream.astype(jnp.bfloat16)[None], (planes, rows, chunk))
    whole = lax.all_to_all(sent, XY, split_axis=0, concat_axis=0, tiled=True)
    whole = whole.transpose(1, 0, 2).reshape(rows, width).astype(jnp.float32)
    factor = lax.rsqrt(jnp.mean(whole * whole, axis=1, keepdims=True) + 1e-05)
    normed = (whole * factor * norm_gain.astype(jnp.float32)).astype(jnp.bfloat16)
    gate = jnp.einsum("bd,fd->bf", normed, gate_weight, preferred_element_type=jnp.float32)
    upward = jnp.einsum("bd,fd->bf", normed, up_weight, preferred_element_type=jnp.float32)
    hidden = (jax.nn.silu(gate) * upward).astype(jnp.bfloat16)
    devices = lax.axis_size(ALL)
    share = width // devices
    down = jnp.dot(hidden, down_weight, preferred_element_type=jnp.float32)
    down = down.astype(jnp.bfloat16).reshape(rows, devices, share).transpose(1, 0, 2)
    down = lax.all_to_all(down, ALL, split_axis=0, concat_axis=0, tiled=True)
    down = jnp.sum(down.astype(jnp.float32), axis=0)
    own = lax.dynamic_slice_in_dim(stream, lax.axis_index(("c", "z")) * share, share, 1)
    return (own + down).astype(jnp.bfloat16)


def solution(mesh):
    fine = Mesh(mesh.devices.reshape(4, 4, 2, 4), ALL)
    placed = (
        P(None, "z", None),
        P(None, KV, "z", None),
        P(None, KV, "z", None),
        P(),
        P(),
        P(("z",) + KV, None),
        P(),
        P(ALL, None),
        P(ALL, None),
        P(ALL, None),
    )
    return jax.shard_map(per_device, mesh=fine, in_specs=placed, out_specs=P(None, ALL), check_vma=False)
```

time: 860 us -> 104 us (0.12)
  waiting for transfers between devices: 803 us -> 29.2 us
  blocking collectives: 0 us -> 31.2 us
  between operations: 13.5 us -> 0.17 us
    reduce_scatter x1 -> x0, waiting for transfers between devices: 637 us -> none  [per_device(): lax.psum_scatter(block_term(hidden, down_weight, share_width, lax.axis_si...]
    psum x1 -> x0, waiting for transfers between devices: 146 us -> none  [per_device(): lax.psum(projected, ('kv', 'head'))]
    all_to_all x0 -> x2, blocking collectives: none -> 31.2 us  [the longest x1 16.1 us: per_device(): came = lax.all_to_all(message, KV, split_axis=0, concat_axis=0, tiled=True)]
    all_to_all x3 -> x2, waiting for transfers between devices: 20.3 us -> 23.3 us  [the longest x1 13.3 us: per_device(): down = lax.all_to_all(down, ALL, split_axis=0, concat_axis=0, tiled=True)]
where the time goes in v1:
time: 104 us; the launch traced here: 103 us
  blocking collectives  31.2 us (30%)
  waiting for transfers between devices  29.2 us (28%)
  matrix products  19.1 us (18%)
  starting transfers between devices  16.4 us (16%)
  other arithmetic  3.68 us (4%)
  local copies, waits for them, and re-layouts  3.02 us (3%)
    all_to_all x1, blocking collectives, per_device(): came = lax.all_to_all(message, KV, split_axis=0, concat_axis=0, tiled=True)  16.1 us
    all_to_all x1, blocking collectives, per_device(): pieces = lax.all_to_all(pieces, XY, split_axis=0, concat_axis=0, tiled=True)  15 us
    all_to_all x1, waiting for transfers between devices, per_device(): down = lax.all_to_all(down, ALL, split_axis=0, concat_axis=0, tiled=True)  13.3 us
    all_to_all x1, waiting for transfers between devices, per_device(): whole = lax.all_to_all(sent, XY, split_axis=0, concat_axis=0, tiled=True)  10 us
    dot_general x1, matrix products, per_device(): down = jnp.dot(hidden, down_weight, preferred_element_type=jnp.float32)  9.5 us
    all_to_all x1, starting transfers between devices, per_device(): down = lax.all_to_all(down, ALL, split_axis=0, concat_axis=0, tiled=True)  6.67 us
    ppermute x3, starting transfers between devices, exchange(): return lax.ppermute(block, axis, [(i, i ^ flip) for i in range(size)])  6.13 us
    ppermute x3, waiting for transfers between devices, exchange(): return lax.ppermute(block, axis, [(i, i ^ flip) for i in range(size)])  5.9 us
  transfers between devices with their start and end apart: 5, of which 5 were waited for; matrix products, arithmetic and copies ran while one was open for 0% of the time, Pallas kernels for 0%

profile of v1, /device:TPU:0, one launch (start us, length us, event | category | flops | bytes accessed | tf_op | source)
XLA Modules:
  0.0 102.7 jit_solution(51911743581708061)
XLA Ops:
  0.0 0.8 broadcast_compare_fusion
  0.8 1.6 %fusion.25 = (bf16[16,2,16]{2,1,0:T(2,128)(2,1)S(1)}, f32[16,2,16,64]{3,2,1,0:T(8,128)S(1)}) fusion(bf16[16,2,16,128]{3,2,1,0:T(8,128)(2,1)} %bitcast.36, bf16[16,64,2,128]{3,2,1,0:T(2,128)(2,1)} %param.11, pred[16,64]{1,0:T(8,128)(4,1)S(1)} %broadcast_compare_fusion), kind=kOutput, calls=%fused_computation.49 | convolution fusion | flops 8486400 | bytes 788480 | tf_op jit(solution)/shard_map/bkgd,bskd->bkgs/dot_general | solution.py:18
  2.5 0.3 fusion.6
  2.8 0.3 convolution_convert_fusion.2
  3.2 0.1 broadcast_in_dim.45
  3.4 0.1 broadcast_in_dim.44
  3.7 16.1 %all_to_all.20 = bf16[32,32,128]{2,1,0:T(8,128)(2,1)S(1)} all-to-all(bf16[32,32,128]{2,1,0:T(8,128)(2,1)S(1)} %bitcast.35), channel_id=1, replica_groups=mesh['x'=4,'y'=4,'c'=2,'z'=4] {'x','y','c'}, dimensions={0} | all-to-all | bytes 524288 | tf_op jit(solution)/shard_map/all_to_all | solution.py:59
  19.9 0.2 fusion.24
  20.0 0.2 copy.28
  20.3 0.2 copy.27
  20.5 0.2 multiply_reduce_fusion.1
  20.7 0.1 multiply_reduce_fusion
  21.0 2.9 %convolution_convert_fusion.1 = bf16[16,16384]{1,0:T(8,128)(2,1)S(1)} fusion(bf16[128,16384]{1,0:T(8,128)(2,1)} %param.15, f32[16,128]{0,1:T(8,128)S(1)} %copy.26, f32[16]{0:T(128)S(1)} %get-tuple-element.10), kind=kOutput, calls=%fused_computation.1 | convolution fusion | flops 67375104 | bytes 4726848 | tf_op jit(solution)/shard_map/dot_general | solution.py:63
  23.9 15.0 %all_to_all.21 = bf16[16,16,1024]{2,1,0:T(8,128)(2,1)S(1)} all-to-all(bf16[16,16,1024]{2,1,0:T(8,128)(2,1)S(1)} %bitcast.34), channel_id=1, replica_groups=mesh['x'=4,'y'=4,'c'=2,'z'=4] {'x','y'}, dimensions={0} | all-to-all | bytes 1048576 | tf_op jit(solution)/shard_map/all_to_all | solution.py:65
  39.1 1.2 %collective-permute-done = f32[16,1024]{1,0:T(8,128)S(1)} collective-permute-done((f32[16,1024]{1,0:T(8,128)S(1)}, f32[16,1024]{1,0:T(8,128)S(1)}, u32[]{:S(2)}, u32[]{:S(2)}) %collective-permute-start) | collective-permute-done | bytes 65568 | tf_op jit(solution)/shard_map/ppermute | solution.py:50
  40.4 2.0 %collective-permute-start.1 = (f32[16,1024]{1,0:T(8,128)S(1)}, f32[16,1024]{1,0:T(8,128)S(1)}, u32[]{:S(2)}, u32[]{:S(2)}) collective-permute-start(f32[16,1024]{1,0:T(8,128)S(1)} %add.59), channel_id=1, source_target_pairs={{0,1},{1,0},{2,3},{3,2},{4,5},{5,4},{6,7},{7,6},{8,9},{9,8},{10,11... | collective-permute-start | bytes 196616 | tf_op jit(solution)/shard_map/ppermute | solution.py:50
  42.3 2.4 %collective-permute-done.1 = f32[16,1024]{1,0:T(8,128)S(1)} collective-permute-done((f32[16,1024]{1,0:T(8,128)S(1)}, f32[16,1024]{1,0:T(8,128)S(1)}, u32[]{:S(2)}, u32[]{:S(2)}) %collective-permute-start.1) | collective-permute-done | bytes 65568 | tf_op jit(solution)/shard_map/ppermute | solution.py:50
  44.8 4.0 %collective-permute-start.2 = (f32[16,1024]{1,0:T(8,128)S(1)}, f32[16,1024]{1,0:T(8,128)S(1)}, u32[]{:S(2)}, u32[]{:S(2)}) collective-permute-start(f32[16,1024]{1,0:T(8,128)S(1)} %add.60), channel_id=1, source_target_pairs={{0,3},{1,2},{2,1},{3,0},{4,7},{5,6},{6,5},{7,4},{8,11},{9,10},{10,... | collective-permute-start | bytes 196616 | tf_op jit(solution)/shard_map/ppermute | solution.py:50
  48.8 2.2 %collective-permute-done.2 = f32[16,1024]{1,0:T(8,128)S(1)} collective-permute-done((f32[16,1024]{1,0:T(8,128)S(1)}, f32[16,1024]{1,0:T(8,128)S(1)}, u32[]{:S(2)}, u32[]{:S(2)}) %collective-permute-start.2) | collective-permute-done | bytes 65568 | tf_op jit(solution)/shard_map/ppermute | solution.py:50
  51.1 0.8 fusion.23
  51.8 0.8 broadcast_in_dim.46
  52.7 3.6 %all-to-all-start.2 = ((bf16[16,16,1024]{2,1,0:T(8,128)(2,1)}), bf16[16,16,1024]{2,1,0:T(8,128)(2,1)S(1)}, u32[]{:S(2)}, u32[]{:S(2)}) async-start(bf16[16,16,1024]{2,1,0:T(8,128)(2,1)} %broadcast_in_dim.46), calls=%async_computation.2 | async-start | bytes 1048576 | tf_op jit(solution)/shard_map/all_to_all | solution.py:73
  56.3 10.0 %all-to-all-done.2 = bf16[16,16,1024]{2,1,0:T(8,128)(2,1)S(1)} async-done(((bf16[16,16,1024]{2,1,0:T(8,128)(2,1)}), bf16[16,16,1024]{2,1,0:T(8,128)(2,1)S(1)}, u32[]{:S(2)}, u32[]{:S(2)}) %all-to-all-start.2) | async-done | bytes 524320 | tf_op jit(solution)/shard_map/all_to_all | solution.py:73
  66.3 0.2 fusion.3
  66.6 0.1 convert_bitcast_fusion
  66.8 4.8 %fusion.22 = f32[16,208]{1,0:T(8,128)S(1)} fusion(bf16[208,16384]{1,0:T(8,128)(2,1)} %param.17, f32[16,16384]{1,0:T(8,128)S(1)} %bitcast.31, f32[16384]{0:T(1024)S(1)} %convert_element_type.116, f32[16]{0:T(128)S(1)} %add_rsqrt_fusion), kind=kOutput, calls=%fused_computation.46 | convolution fusion | flops 109838336 | bytes 7943232 | tf_op jit(solution)/shard_map/bd,fd->bf/dot_general | solution.py:77
  71.6 9.5 %fusion = bf16[2,128,8,128]{3,2,1,0:T(8,128)(2,1)S(1)} fusion(bf16[208,16384]{1,0:T(8,128)(2,1)} %param.19, bf16[208,16384]{1,0:T(8,128)(2,1)} %param.18, f32[16,208]{1,0:T(8,128)S(1)} %fusion.22, f32[16,16384]{1,0:T(8,128)S(1)} %bitcast.32, f32[16384]{0:T(1024)S(1)} %convert_element_type.116, f32[16]{0:T(128)S(1)} %add_rsqrt_fusion), kind=kOutput, calls=%fused_computation.4 | convolution fusion | flops 219172352 | bytes 15283264 | tf_op jit(solution)/shard_map/dot_general | solution.py:82
  81.1 0.9 copy.42
  82.0 6.7 %all-to-all-start.3 = ((bf16[128,16,128]{2,1,0:T(8,128)(2,1)}), bf16[128,16,128]{2,1,0:T(8,128)(2,1)S(1)}, u32[]{:S(2)}, u32[]{:S(2)}) async-start(bf16[128,16,128]{2,1,0:T(8,128)(2,1)} %bitcast.27), calls=%async_computation.3 | async-start | bytes 1048576 | tf_op jit(solution)/shard_map/all_to_all | solution.py:84
  88.7 13.3 %all-to-all-done.3 = bf16[128,16,128]{2,1,0:T(8,128)(2,1)S(1)} async-done(((bf16[128,16,128]{2,1,0:T(8,128)(2,1)}), bf16[128,16,128]{2,1,0:T(8,128)(2,1)S(1)}, u32[]{:S(2)}, u32[]{:S(2)}) %all-to-all-start.3) | async-done | bytes 524320 | tf_op jit(solution)/shard_map/all_to_all | solution.py:84
  102.0 0.1 convert_reduce_fusion
  102.1 0.6 add_convert_fusion
  (21 shorter events, 0.9 us)
Async XLA Ops:
  0.0 2.8 %copy-start = (bf16[16,64,2,128]{3,2,1,0:T(2,128)(2,1)S(1)}, bf16[16,64,2,128]{3,2,1,0:T(2,128)(2,1)}, u32[]{:S(2)}) copy-start(bf16[16,64,2,128]{3,2,1,0:T(2,128)(2,1)} %param.12) | copy-start | bytes 1572868
  2.8 53.5 %copy-start.1 = (bf16[16384]{0:T(1024)(128)(2,1)S(1)}, bf16[16384]{0:T(1024)(128)(2,1)}, u32[]{:S(2)}) copy-start(bf16[16384]{0:T(1024)(128)(2,1)} %param.16) | copy-start | bytes 98308
  39.0 1.3 %collective-permute-start = (f32[16,1024]{1,0:T(8,128)S(1)}, f32[16,1024]{1,0:T(8,128)S(1)}, u32[]{:S(2)}, u32[]{:S(2)}) collective-permute-start(f32[16,1024]{1,0:T(8,128)S(1)} %convert_reduce_fusion.1), channel_id=1, source_target_pairs={{0,4},{4,0},{1,5},{5,1},{2,6},{6,2},{3,7},{7,3},{8,12},{12,8},{9,1... | collective-permute-start | bytes 196616 | tf_op jit(solution)/shard_map/ppermute | solution.py:50
  40.4 4.4 %collective-permute-start.1 = (f32[16,1024]{1,0:T(8,128)S(1)}, f32[16,1024]{1,0:T(8,128)S(1)}, u32[]{:S(2)}, u32[]{:S(2)}) collective-permute-start(f32[16,1024]{1,0:T(8,128)S(1)} %add.59), channel_id=1, source_target_pairs={{0,1},{1,0},{2,3},{3,2},{4,5},{5,4},{6,7},{7,6},{8,9},{9,8},{10,11... | collective-permute-start | bytes 196616 | tf_op jit(solution)/shard_map/ppermute | solution.py:50
  44.8 6.3 %collective-permute-start.2 = (f32[16,1024]{1,0:T(8,128)S(1)}, f32[16,1024]{1,0:T(8,128)S(1)}, u32[]{:S(2)}, u32[]{:S(2)}) collective-permute-start(f32[16,1024]{1,0:T(8,128)S(1)} %add.60), channel_id=1, source_target_pairs={{0,3},{1,2},{2,1},{3,0},{4,7},{5,6},{6,5},{7,4},{8,11},{9,10},{10,... | collective-permute-start | bytes 196616 | tf_op jit(solution)/shard_map/ppermute | solution.py:50
  52.7 13.6 %all-to-all-start.2 = ((bf16[16,16,1024]{2,1,0:T(8,128)(2,1)}), bf16[16,16,1024]{2,1,0:T(8,128)(2,1)S(1)}, u32[]{:S(2)}, u32[]{:S(2)}) async-start(bf16[16,16,1024]{2,1,0:T(8,128)(2,1)} %broadcast_in_dim.46), calls=%async_computation.2 | async-start | bytes 1048576 | tf_op jit(solution)/shard_map/all_to_all | solution.py:73
  82.0 20.0 %all-to-all-start.3 = ((bf16[128,16,128]{2,1,0:T(8,128)(2,1)}), bf16[128,16,128]{2,1,0:T(8,128)(2,1)S(1)}, u32[]{:S(2)}, u32[]{:S(2)}) async-start(bf16[128,16,128]{2,1,0:T(8,128)(2,1)} %bitcast.27), calls=%async_computation.3 | async-start | bytes 1048576 | tf_op jit(solution)/shard_map/all_to_all | solution.py:84

commit v2 on v1

v2 whole, which is shorter than its diff:
```python
import functools

import jax
import jax.numpy as jnp
from jax import lax
from jax.experimental import pallas as pl
from jax.experimental.pallas import tpu as pltpu
from jax.sharding import Mesh, PartitionSpec as P

KV = ("x", "y", "c")
ALL = ("x", "y", "c", "z")
LANES = 128
MIB = 2**20
LAST = (((1,), (1,)), ((), ()))
FIRST = (((0,), (0,)), ((), ()))


def flat_index(axes):
    index = 0
    for axis in axes:
        index = index * lax.axis_size(axis) + lax.axis_index(axis)
    return index


def call(kernel, outs, args, spaces, scratch=(), limit=16 * MIB, flops=0):
    shapes = [jax.ShapeDtypeStruct(*out) for out in outs]
    specs = [pl.BlockSpec(memory_space=pltpu.VMEM)] * len(outs)
    return pl.pallas_call(
        kernel,
        out_shape=shapes,
        in_specs=[pl.BlockSpec(memory_space=space) for space in spaces],
        out_specs=specs,
        scratch_shapes=list(scratch),
        compiler_params=pltpu.CompilerParams(vmem_limit_bytes=limit),
        cost_estimate=pl.CostEstimate(flops=flops, bytes_accessed=MIB, transcendentals=0),
    )(*args)


def attention_kernel(
    groups,
    lengths_hbm,
    q_hbm,
    k_hbm,
    v_hbm,
    weight_hbm,
    residual_hbm,
    message_ref,
    weight_ref,
    residual_ref,
    lengths_ref,
    q_ref,
    k_ref,
    v_ref,
    held,
    sems,
):
    rows, heads, width = q_ref.shape
    slots = k_ref.shape[1]
    span = slots // groups
    size = heads // groups
    height = message_ref.shape[1]
    columns = pl.ds(pl.multiple_of(flat_index(ALL) * LANES, LANES), LANES)
    loads = [
        pltpu.make_async_copy(source, target, sems.at[i])
        for i, (source, target) in enumerate(
            (
                (q_hbm, q_ref),
                (k_hbm, k_ref),
                (lengths_hbm, lengths_ref),
                (v_hbm, v_ref),
                (weight_hbm, weight_ref),
                (residual_hbm.at[:, columns], residual_ref),
            )
        )
    ]
    for load in loads:
        load.start()
    base = flat_index(KV) * span
    head = lax.broadcasted_iota(jnp.int32, (heads, slots), 0)
    slot = lax.broadcasted_iota(jnp.int32, (heads, slots), 1)
    own = (head // size) == (slot % groups)
    position = jnp.where(own, base + slot // groups, jnp.int32(2**30))
    lane = lax.broadcasted_iota(jnp.int32, (heads, width), 1)
    half = width // 2
    for load in loads[:3]:
        load.wait()
    scores = [
        lax.dot_general(q_ref[b], k_ref[b], LAST, preferred_element_type=jnp.float32) * width ** (-0.5)
        for b in range(rows)
    ]
    weights, packed = [], []
    for b in range(rows):
        live = position < lengths_ref[b]
        masked = jnp.where(live, scores[b], -1e30)
        point = jnp.max(masked, axis=1, keepdims=True).astype(jnp.bfloat16).astype(jnp.float32)
        weight = jnp.where(live, jnp.exp(masked - point), 0.0)
        weights.append(weight.astype(jnp.bfloat16))
        packed.append((point, jnp.sum(weight, axis=1, keepdims=True)))
    loads[3].wait()
    outs = [jnp.dot(weights[b], v_ref[b], preferred_element_type=jnp.float32) for b in range(rows)]
    for b in range(rows):
        held[pl.ds(b, heads, stride=height), :] = outs[b]
    for b in range(rows // 2):
        (point, total), (later_point, later_total) = packed[b], packed[b + rows // 2]
        stats = jnp.where(
            lane < half,
            jnp.where(lane < half // 2, point, total),
            jnp.where(lane < half + half // 2, later_point, later_total),
        )
        held[pl.ds(rows + b, heads, stride=height), :] = stats
    for h in range(heads):
        message_ref[h] = held[h * height : (h + 1) * height, :].astype(jnp.bfloat16)
    loads[4].wait()
    loads[5].wait()


def attention(lengths, queries, k_cache, v_cache, weight, residual):
    rows, heads, width = queries.shape
    span, groups = k_cache.shape[1:3]
    height = rows + rows // 2
    cache = (rows, span * groups, width)
    return call(
        functools.partial(attention_kernel, groups),
        [
            ((heads, height, width), jnp.bfloat16),
            (weight.shape, jnp.bfloat16),
            ((rows, LANES), jnp.bfloat16),
        ],
        [
            pltpu.with_memory_space_constraint(a, pltpu.HBM)
            for a in (lengths, queries, k_cache.reshape(cache), v_cache.reshape(cache), weight, residual)
        ],
        [pltpu.HBM] * 6,
        [
            pltpu.SMEM(lengths.shape, jnp.int32),
            pltpu.VMEM(queries.shape, jnp.bfloat16),
            pltpu.VMEM(cache, jnp.bfloat16),
            pltpu.VMEM(cache, jnp.bfloat16),
            pltpu.VMEM((heads * height, width), jnp.float32),
            pltpu.SemaphoreType.DMA((6,)),
        ],
        limit=12 * MIB,
    )


def project_kernel(rows, step, came_ref, weight_ref, out_ref):
    parts, _, width = came_ref.shape
    half = width // 2
    stats = came_ref[:, rows:, :].astype(jnp.float32)
    point = jnp.concatenate([stats[:, :, :1], stats[:, :, half : half + 1]], axis=1)
    quarter = half // 2
    total = jnp.concatenate(
        [stats[:, :, quarter : quarter + 1], stats[:, :, half + quarter : half + quarter + 1]], axis=1
    )
    scale = jnp.exp(point - jnp.max(point, axis=0, keepdims=True))
    out = jnp.sum(scale * came_ref[:, :rows, :].astype(jnp.float32), axis=0)
    attended = (out / jnp.sum(scale * total, axis=0)).astype(jnp.bfloat16)
    for at in range(0, weight_ref.shape[1], step):
        product = jnp.dot(attended, weight_ref[:, at : at + step], preferred_element_type=jnp.float32)
        for j in range(step // LANES):
            out_ref[at // LANES + j] = product[:, j * LANES : (j + 1) * LANES].astype(jnp.bfloat16)


def project(came, weight, rows, step=2048):
    pieces = weight.shape[1] // LANES
    return call(
        functools.partial(project_kernel, rows, step),
        [((pieces, rows, LANES), jnp.bfloat16)],
        [came, weight],
        [pltpu.VMEM] * 2,
        limit=12 * MIB,
        flops=10**10,
    )[0]


def stream_kernel(came_ref, residual_ref, stream_ref, sent_ref):
    total = jnp.sum(came_ref[...].astype(jnp.float32), axis=0)
    stream = total + residual_ref[...].astype(jnp.float32)
    stream_ref[...] = stream
    sent_ref[...] = jnp.broadcast_to(stream.astype(jnp.bfloat16)[None], sent_ref.shape)


def stream_sum(came, residual):
    shape = came.shape
    return call(
        stream_kernel,
        [(shape[1:], jnp.float32), (shape, jnp.bfloat16)],
        [came, residual],
        [pltpu.VMEM] * 2,
    )


def feed_forward_kernel(step, whole_ref, gain_ref, gate_ref, up_ref, down_ref, out_ref):
    pieces, rows, _ = whole_ref.shape
    units, width = gate_ref.shape
    per = step // LANES
    gate = jnp.zeros((units, rows), jnp.float32)
    up = jnp.zeros((units, rows), jnp.float32)
    square = jnp.zeros((rows, LANES), jnp.float32)
    for k in range(width // step):
        parts = []
        for j in range(k * per, (k + 1) * per):
            part = whole_ref[j].astype(jnp.float32)
            square += part * part
            parts.append((part * gain_ref[j : j + 1, :].astype(jnp.float32)).astype(jnp.bfloat16))
        block = jnp.concatenate(parts, axis=1)
        columns = slice(k * step, (k + 1) * step)
        gate += lax.dot_general(gate_ref[:, columns], block, LAST, preferred_element_type=jnp.float32)
        up += lax.dot_general(up_ref[:, columns], block, LAST, preferred_element_type=jnp.float32)
    factor = lax.rsqrt(jnp.sum(square.T, axis=0, keepdims=True) * (1.0 / width) + 1e-05)
    gate = gate * factor
    hidden = (gate / (1.0 + jnp.exp(-gate)) * (up * factor)).T.astype(jnp.bfloat16)
    for k in range(width // step):
        product = jnp.dot(hidden, down_ref[:, k * step : (k + 1) * step], preferred_element_type=jnp.float32)
        for j in range(per):
            out_ref[k * per + j] = product[:, j * LANES : (j + 1) * LANES].astype(jnp.bfloat16)


def feed_forward(whole, gain, gate, up, down, step=2048):
    return call(
        functools.partial(feed_forward_kernel, step),
        [(whole.shape, jnp.bfloat16)],
        [whole, gain.reshape(-1, LANES), gate, up, down],
        [pltpu.VMEM] * 5,
        limit=30 * MIB,
    )[0]


def swap(blocks, axes):
    return lax.all_to_all(blocks, axes, split_axis=0, concat_axis=0, tiled=True)


def per_device(
    queries, k_cache, v_cache, lengths, residual_in, out_weight, norm_gain, gate_weight, up_weight, down_weight
):
    rows = queries.shape[0]
    message, weight, residual = attention(lengths, queries, k_cache, v_cache, out_weight, residual_in)
    came = swap(message, KV)
    stream, sent = stream_sum(swap(project(came, weight, rows), ALL), residual)
    whole = swap(sent, ALL)
    down = swap(feed_forward(whole, norm_gain, gate_weight, up_weight, down_weight), ALL)
    return (stream + jnp.sum(down.astype(jnp.float32), axis=0)).astype(jnp.bfloat16)


def solution(mesh):
    fine = Mesh(mesh.devices.reshape(4, 4, 2, 4), ALL)
    placed = (
        P(None, "z", None),
        P(None, KV, "z", None),
        P(None, KV, "z", None),
        P(),
        P(),
        P(("z",) + KV, None),
        P(),
        P(ALL, None),
        P(ALL, None),
        P(ALL, None),
    )
    return jax.shard_map(per_device, mesh=fine, in_specs=placed, out_specs=P(None, ALL), check_vma=False)
```

time: 104 us -> 82.7 us (0.80)
  blocking collectives: 31.2 us -> 72.2 us
  waiting for transfers between devices: 29.2 us -> 0 us
  matrix products: 19.1 us -> 0 us
  starting transfers between devices: 16.4 us -> 0 us
  Pallas kernels: 0 us -> 8.53 us
  local copies, waits for them, and re-layouts: 3.02 us -> 0.03 us
  other arithmetic: 3.68 us -> 0.74 us
    all_to_all x2 -> x4, blocking collectives: 31.2 us -> 72.2 us  [swap(): return lax.all_to_all(blocks, axes, split_axis=0, concat_axis=0, tiled=True)]
    all_to_all x2 -> x0, waiting for transfers between devices: 23.3 us -> none  [the longest x1 13.3 us: per_device(): down = lax.all_to_all(down, ALL, split_axis=0, concat_axis=0, tiled=True)]
    dot_general x5 -> x0, matrix products: 19.1 us -> none  [the longest x1 9.5 us: per_device(): down = jnp.dot(hidden, down_weight, preferred_element_type=jnp.float32)]
    all_to_all x2 -> x0, starting transfers between devices: 10.2 us -> none  [the longest x1 6.67 us: per_device(): down = lax.all_to_all(down, ALL, split_axis=0, concat_axis=0, tiled=True)]
    pallas_call x0 -> x4, Pallas kernels: none -> 8.53 us  [call(): pl.pallas_call(kernel, out_shape=shapes, in_specs=[pl.BlockSpec(memory_sp...]
    ppermute x3 -> x0, starting transfers between devices: 6.13 us -> none  [exchange(): return lax.ppermute(block, axis, [(i, i ^ flip) for i in range(size)])]
    ppermute x3 -> x0, waiting for transfers between devices: 5.9 us -> none  [exchange(): return lax.ppermute(block, axis, [(i, i ^ flip) for i in range(size)])]
    broadcast_in_dim x3 -> x0, local copies, waits for them, and re-layouts: 1.12 us -> none  [the longest x1 0.85 us: per_device(): jnp.broadcast_to(stream.astype(jnp.bfloat16)[None], (planes, rows, chunk))]
  transfers between devices with their start and end apart: 5 -> 0, of which waited for: 5 -> 0; matrix products, arithmetic and copies ran while one was open for 0% -> 0% of each run, Pallas kernels for 0% -> 0%
where the time goes in v2:
time: 82.7 us; the launch traced here: 81.5 us
  blocking collectives  72.2 us (87%)
  Pallas kernels  8.53 us (10%)
    all_to_all x4, blocking collectives, swap(): return lax.all_to_all(blocks, axes, split_axis=0, concat_axis=0, tiled=True)  72.2 us
    pallas_call x4, Pallas kernels, call(): pl.pallas_call(kernel, out_shape=shapes, in_specs=[pl.BlockSpec(memory_sp...  8.53 us

profile of v2, /device:TPU:0, one launch (start us, length us, event | category | flops | bytes accessed | tf_op | source)
XLA Modules:
  0.0 81.5 jit_solution(16690060105416086129)
XLA Ops:
  0.0 0.0 slice-start
  0.0 0.0 slice-start.2
  0.0 0.0 slice-start.4
  0.0 2.8 %shard_map.100 = (bf16[32,24,128]{2,1,0:T(8,128)(2,1)S(1)}, bf16[128,16384]{1,0:T(8,128)(2,1)S(1)}, bf16[16,128]{1,0:T(8,128)(2,1)S(1)}) custom-call(s32[16]{0:T(128)} %lengths_hbm.1, bf16[16,32,128]{2,1,0:T(8,128)(2,1)} %q_hbm.1, bf16[16,128,128]{2,1,0:T(8,128)(2,1)} %bitcast.10, bf16[16,128,128]{2,1,0:T(8,128)(2,1)} %bitcast.11, ...), custom_call_target="tpu_custom_call" | custom-call | bytes 1048576 | tf_op jit(solution)/shard_map/pallas_call | solution.py:28
  2.8 15.8 %all_to_all.20.came_ref = bf16[32,24,128]{2,1,0:T(8,128)(2,1)S(1)} all-to-all(bf16[32,24,128]{2,1,0:T(8,128)(2,1)S(1)} %get-tuple-element.10), channel_id=1, replica_groups=mesh['x'=4,'y'=4,'c'=2,'z'=4] {'x','y','c'}, dimensions={0} | all-to-all | bytes 393216 | tf_op jit(solution)/shard_map/all_to_all | solution.py:230
  18.6 0.0 slice-start.1
  18.6 0.0 slice-start.3
  18.6 0.0 slice-start.5
  18.6 0.0 copy-start
  18.6 0.9 %shard_map.101 = bf16[128,16,128]{2,1,0:T(8,128)(2,1)S(1)} custom-call(bf16[32,24,128]{2,1,0:T(8,128)(2,1)S(1)} %all_to_all.20.came_ref, bf16[128,16384]{1,0:T(8,128)(2,1)S(1)} %get-tuple-element.11.weight_ref), custom_call_target="tpu_custom_call" | custom-call | flops 10000000000 | bytes 1048576 | tf_op jit(solution)/shard_map/pallas_call | solution.py:28
  19.5 20.6 %all_to_all.21.came_ref = bf16[128,16,128]{2,1,0:T(8,128)(2,1)S(1)} all-to-all(bf16[128,16,128]{2,1,0:T(8,128)(2,1)S(1)} %shard_map.101), channel_id=1, replica_groups=mesh['x'=4,'y'=4,'c'=2,'z'=4] {'x','y','c','z'}, dimensions={0} | all-to-all | bytes 1048576 | tf_op jit(solution)/shard_map/all_to_all | solution.py:230
  40.1 0.2 shard_map.102
  40.3 17.9 %all_to_all.22.whole_ref = bf16[128,16,128]{2,1,0:T(8,128)(2,1)S(1)} all-to-all(bf16[128,16,128]{2,1,0:T(8,128)(2,1)S(1)} %get-tuple-element.14), channel_id=1, replica_groups=mesh['x'=4,'y'=4,'c'=2,'z'=4] {'x','y','c','z'}, dimensions={0} | all-to-all | bytes 1048576 | tf_op jit(solution)/shard_map/all_to_all | solution.py:230
  58.2 0.0 slice-done
  58.2 0.0 slice-done.2
  58.2 0.0 slice-done.4
  58.2 0.0 slice-done.1
  58.2 0.0 slice-done.3
  58.2 0.0 slice-done.5
  58.2 0.0 copy-done
  58.3 4.7 %shard_map.103 = bf16[128,16,128]{2,1,0:T(8,128)(2,1)S(1)} custom-call(bf16[128,16,128]{2,1,0:T(8,128)(2,1)S(1)} %all_to_all.22.whole_ref, bf16[128,128]{1,0:T(8,128)(2,1)S(1)} %bitcast.9, bf16[208,16384]{1,0:T(8,128)(2,1)S(1)} %bitcast.4, bf16[208,16384]{1,0:T(8,128)(2,1)S(1)} %bitcast.6, bf16[208,16384]{1,0:T(8,128)(2,1)S(1)} %bitcast.8), custom_call_target="tpu_custom_call" | custom-call | bytes 1048576 | tf_op jit(solution)/shard_map/pallas_call | solution.py:28
  62.9 17.9 %all_to_all.23 = bf16[128,16,128]{2,1,0:T(8,128)(2,1)S(1)} all-to-all(bf16[128,16,128]{2,1,0:T(8,128)(2,1)S(1)} %shard_map.103), channel_id=1, replica_groups=mesh['x'=4,'y'=4,'c'=2,'z'=4] {'x','y','c','z'}, dimensions={0} | all-to-all | bytes 1048576 | tf_op jit(solution)/shard_map/all_to_all | solution.py:230
  80.8 0.1 convert_reduce_fusion
  80.9 0.6 add_convert_fusion
  (3 shorter events, 0.0 us)
Async XLA Ops:
  0.0 58.2 %slice-start = ((s8[6815744]{0:T(1024)(128)(4,1)}), s8[4194304]{0:T(1024)(128)(4,1)S(1)}, s32[]{:S(2)}) async-start(s8[6815744]{0:T(1024)(128)(4,1)} %bitcast.3), calls=%async_computation.4 | async-start | bytes 8388608
  0.0 58.2 %slice-start.2 = ((s8[6815744]{0:T(1024)(128)(4,1)}), s8[4194304]{0:T(1024)(128)(4,1)S(1)}, s32[]{:S(2)}) async-start(s8[6815744]{0:T(1024)(128)(4,1)} %bitcast.5), calls=%async_computation.6 | async-start | bytes 8388608
  0.0 58.2 %slice-start.4 = ((s8[6815744]{0:T(1024)(128)(4,1)}), s8[4194304]{0:T(1024)(128)(4,1)S(1)}, s32[]{:S(2)}) async-start(s8[6815744]{0:T(1024)(128)(4,1)} %bitcast.7), calls=%async_computation.8 | async-start | bytes 8388608
  18.6 39.6 %slice-start.1 = ((s8[6815744]{0:T(1024)(128)(4,1)}), s8[2621440]{0:T(1024)(128)(4,1)S(1)}, s32[]{:S(2)}) async-start(s8[6815744]{0:T(1024)(128)(4,1)} %bitcast.3), calls=%async_computation.5 | async-start | bytes 5242880
  18.6 39.6 %slice-start.3 = ((s8[6815744]{0:T(1024)(128)(4,1)}), s8[2621440]{0:T(1024)(128)(4,1)S(1)}, s32[]{:S(2)}) async-start(s8[6815744]{0:T(1024)(128)(4,1)} %bitcast.5), calls=%async_computation.7 | async-start | bytes 5242880
  18.6 39.6 %slice-start.5 = ((s8[6815744]{0:T(1024)(128)(4,1)}), s8[2621440]{0:T(1024)(128)(4,1)S(1)}, s32[]{:S(2)}) async-start(s8[6815744]{0:T(1024)(128)(4,1)} %bitcast.7), calls=%async_computation.9 | async-start | bytes 5242880
  18.6 39.6 %copy-start = (bf16[16384]{0:T(1024)(128)(2,1)S(1)}, bf16[16384]{0:T(1024)(128)(2,1)}, u32[]{:S(2)}) copy-start(bf16[16384]{0:T(1024)(128)(2,1)} %param.16) | copy-start | bytes 98308

commit v3 on v2

--- a/solution.py
+++ b/solution.py
@@ -9,10 +9,10 @@
 
 KV = ("x", "y", "c")
 ALL = ("x", "y", "c", "z")
+CHIPS = ("x", "y", "z")
 LANES = 128
 MIB = 2**20
 LAST = (((1,), (1,)), ((), ()))
-FIRST = (((0,), (0,)), ((), ()))
 
 
 def flat_index(axes):
@@ -143,8 +143,25 @@
     )
 
 
-def project_kernel(rows, step, came_ref, weight_ref, out_ref):
-    parts, _, width = came_ref.shape
+def columns_of(piece, side, run):
+    return pl.ds(pl.multiple_of((2 * piece + side) * run, run), run)
+
+
+def other_core():
+    return 1 - lax.axis_index("c")
+
+
+def half_product(left, weight_ref, side, out_ref):
+    per = lax.axis_size("z")
+    run = per * LANES
+    for piece in range(out_ref.shape[0] // per):
+        product = jnp.dot(left, weight_ref[:, columns_of(piece, side, run)], preferred_element_type=jnp.float32)
+        for j in range(per):
+            out_ref[piece * per + j] = product[:, j * LANES : (j + 1) * LANES].astype(out_ref.dtype)
+
+
+def merge_kernel(rows, came_ref, weight_ref, sent_ref, attended_ref):
+    width = came_ref.shape[2]
     half = width // 2
     stats = came_ref[:, rows:, :].astype(jnp.float32)
     point = jnp.concatenate([stats[:, :, :1], stats[:, :, half : half + 1]], axis=1)
@@ -155,22 +172,44 @@
     scale = jnp.exp(point - jnp.max(point, axis=0, keepdims=True))
     out = jnp.sum(scale * came_ref[:, :rows, :].astype(jnp.float32), axis=0)
     attended = (out / jnp.sum(scale * total, axis=0)).astype(jnp.bfloat16)
-    for at in range(0, weight_ref.shape[1], step):
-        product = jnp.dot(attended, weight_ref[:, at : at + step], preferred_element_type=jnp.float32)
-        for j in range(step // LANES):
-            out_ref[at // LANES + j] = product[:, j * LANES : (j + 1) * LANES].astype(jnp.bfloat16)
-
-
-def project(came, weight, rows, step=2048):
-    pieces = weight.shape[1] // LANES
-    return call(
-        functools.partial(project_kernel, rows, step),
-        [((pieces, rows, LANES), jnp.bfloat16)],
+    attended_ref[...] = attended
+    half_product(attended, weight_ref, other_core(), sent_ref)
+
+
+def merge_and_project(came, weight, rows):
+    chips = weight.shape[1] // LANES // 2
+    return call(
+        functools.partial(merge_kernel, rows),
+        [((chips, rows, LANES), jnp.bfloat16), ((rows, came.shape[2]), jnp.bfloat16)],
         [came, weight],
         [pltpu.VMEM] * 2,
         limit=12 * MIB,
         flops=10**10,
+    )
+
+
+def own_kernel(left_ref, weight_ref, out_ref):
+    half_product(left_ref[...], weight_ref, lax.axis_index("c"), out_ref)
+
+
+def own_half(left, weight):
+    chips = weight.shape[1] // LANES // 2
+    return call(
+        own_kernel,
+        [((chips, left.shape[0], LANES), jnp.float32)],
+        [left, weight],
+        [pltpu.VMEM] * 2,
+        limit=12 * MIB,
+        flops=10**9,
     )[0]
+
+
+def add_kernel(own_ref, came_ref, out_ref):
+    out_ref[...] = (own_ref[...] + came_ref[...].astype(jnp.float32)).astype(jnp.bfloat16)
+
+
+def add(own, came):
+    return call(add_kernel, [(came.shape, jnp.bfloat16)], [own, came], [pltpu.VMEM] * 2)[0]
 
 
 def stream_kernel(came_ref, residual_ref, stream_ref, sent_ref):
@@ -190,56 +229,97 @@
     )
 
 
-def feed_forward_kernel(step, whole_ref, gain_ref, gate_ref, up_ref, down_ref, out_ref):
-    pieces, rows, _ = whole_ref.shape
-    units, width = gate_ref.shape
-    per = step // LANES
-    gate = jnp.zeros((units, rows), jnp.float32)
-    up = jnp.zeros((units, rows), jnp.float32)
-    square = jnp.zeros((rows, LANES), jnp.float32)
-    for k in range(width // step):
+def gate_up(side, whole_ref, gain_ref, gate_ref, up_ref, gate, up, square):
+    per = lax.axis_size("z")
+    run = per * LANES
+    for piece in range(whole_ref.shape[0] // per):
         parts = []
-        for j in range(k * per, (k + 1) * per):
-            part = whole_ref[j].astype(jnp.float32)
+        for j in range(per):
+            part = whole_ref[piece * per + j].astype(jnp.float32)
             square += part * part
-            parts.append((part * gain_ref[j : j + 1, :].astype(jnp.float32)).astype(jnp.bfloat16))
+            gain = gain_ref[pl.ds((2 * piece + side) * per + j, 1), :]
+            parts.append((part * gain).astype(jnp.bfloat16))
         block = jnp.concatenate(parts, axis=1)
-        columns = slice(k * step, (k + 1) * step)
+        columns = columns_of(piece, side, run)
         gate += lax.dot_general(gate_ref[:, columns], block, LAST, preferred_element_type=jnp.float32)
         up += lax.dot_general(up_ref[:, columns], block, LAST, preferred_element_type=jnp.float32)
+    return gate, up, square
+
+
+def first_kernel(whole_ref, gain_ref, gate_ref, up_ref, gate_out, up_out, square_out):
+    zeros = jnp.zeros(gate_out.shape, jnp.float32)
+    gate_out[...], up_out[...], square_out[...] = gate_up(
+        lax.axis_index("c"), whole_ref, gain_ref, gate_ref, up_ref, zeros, zeros, jnp.zeros(square_out.shape, jnp.float32)
+    )
+
+
+def first_half(whole, gain, gate, up):
+    rows, units = whole.shape[1], gate.shape[0]
+    return call(
+        first_kernel,
+        [((units, rows), jnp.float32), ((units, rows), jnp.float32), ((rows, LANES), jnp.float32)],
+        [whole, gain, gate, up],
+        [pltpu.VMEM] * 4,
+        limit=24 * MIB,
+        flops=10**9,
+    )
+
+
+def second_kernel(
+    whole_ref, gain_ref, gate_ref, up_ref, down_ref, gate_sum, up_sum, square_sum, sent_ref, hidden_ref
+):
+    gate, up, square = gate_up(
+        other_core(), whole_ref, gain_ref, gate_ref, up_ref, gate_sum[...], up_sum[...], square_sum[...]
+    )
+    width = gate_ref.shape[1]
     factor = lax.rsqrt(jnp.sum(square.T, axis=0, keepdims=True) * (1.0 / width) + 1e-05)
     gate = gate * factor
     hidden = (gate / (1.0 + jnp.exp(-gate)) * (up * factor)).T.astype(jnp.bfloat16)
-    for k in range(width // step):
-        product = jnp.dot(hidden, down_ref[:, k * step : (k + 1) * step], preferred_element_type=jnp.float32)
-        for j in range(per):
-            out_ref[k * per + j] = product[:, j * LANES : (j + 1) * LANES].astype(jnp.bfloat16)
-
-
-def feed_forward(whole, gain, gate, up, down, step=2048):
-    return call(
-        functools.partial(feed_forward_kernel, step),
-        [(whole.shape, jnp.bfloat16)],
-        [whole, gain.reshape(-1, LANES), gate, up, down],
-        [pltpu.VMEM] * 5,
+    hidden_ref[...] = hidden
+    half_product(hidden, down_ref, other_core(), sent_ref)
+
+
+def second_half(whole, gain, gate, up, down, sums):
+    return call(
+        second_kernel,
+        [(whole.shape, jnp.bfloat16), ((whole.shape[1], gate.shape[0]), jnp.bfloat16)],
+        [whole, gain, gate, up, down, *sums],
+        [pltpu.VMEM] * 8,
         limit=30 * MIB,
-    )[0]
+    )
+
+
+def final_kernel(stream_ref, came_ref, out_ref):
+    total = jnp.sum(came_ref[...].astype(jnp.float32), axis=0)
+    out_ref[...] = (stream_ref[...] + total).astype(jnp.bfloat16)
+
+
+def final_sum(stream, came):
+    return call(final_kernel, [(stream.shape, jnp.bfloat16)], [stream, came], [pltpu.VMEM] * 2)[0]
 
 
 def swap(blocks, axes):
     return lax.all_to_all(blocks, axes, split_axis=0, concat_axis=0, tiled=True)
+
+
+def other(block):
+    return lax.ppermute(block, "c", [(0, 1), (1, 0)])
 
 
 def per_device(
     queries, k_cache, v_cache, lengths, residual_in, out_weight, norm_gain, gate_weight, up_weight, down_weight
 ):
     rows = queries.shape[0]
+    gain = norm_gain.astype(jnp.float32).reshape(-1, LANES)
     message, weight, residual = attention(lengths, queries, k_cache, v_cache, out_weight, residual_in)
-    came = swap(message, KV)
-    stream, sent = stream_sum(swap(project(came, weight, rows), ALL), residual)
-    whole = swap(sent, ALL)
-    down = swap(feed_forward(whole, norm_gain, gate_weight, up_weight, down_weight), ALL)
-    return (stream + jnp.sum(down.astype(jnp.float32), axis=0)).astype(jnp.bfloat16)
+    sent, attended = merge_and_project(swap(message, KV), weight, rows)
+    partial = add(own_half(attended, weight), other(sent))
+    stream, copies = stream_sum(swap(partial, CHIPS), residual)
+    whole = swap(copies, CHIPS)
+    sums = first_half(whole, gain, gate_weight, up_weight)
+    sent, hidden = second_half(other(whole), gain, gate_weight, up_weight, down_weight, sums)
+    partial = add(own_half(hidden, down_weight), other(sent))
+    return final_sum(stream, swap(partial, CHIPS))
 
 
 def solution(mesh):

time: 82.7 us -> 77.6 us (0.938); the launches traced: 81.5 us -> 77.4 us
  blocking collectives: 72.2 us -> 65.4 us
  waiting for transfers between devices: 0 us -> 1.52 us
  starting transfers between devices: 0 us -> 0.89 us
  Pallas kernels: 8.53 us -> 9.41 us
    all_to_all x4, blocking collectives: 72.2 us -> 65.4 us  [swap(): return lax.all_to_all(blocks, axes, split_axis=0, concat_axis=0, tiled=True)]
    ppermute x0 -> x3, waiting for transfers between devices: none -> 1.52 us  [other(): return lax.ppermute(block, 'c', [(0, 1), (1, 0)])]
    ppermute x0 -> x3, starting transfers between devices: none -> 0.89 us  [other(): return lax.ppermute(block, 'c', [(0, 1), (1, 0)])]
    pallas_call x4 -> x10, Pallas kernels: 8.53 us -> 9.41 us  [call(): pl.pallas_call(kernel, out_shape=shapes, in_specs=[pl.BlockSpec(memory_sp...]
  transfers between devices with their start and end apart: 0 -> 3, of which waited for: 0 -> 2; matrix products, arithmetic and copies ran while one was open for 0% -> 0% of each run, Pallas kernels for 0% -> 4%
where the time goes in v3:
time: 77.6 us; the launch traced here: 77.4 us
  blocking collectives  65.4 us (84%)
  Pallas kernels  9.41 us (12%)
  waiting for transfers between devices  1.52 us (2%)
  starting transfers between devices  0.89 us (1%)
    all_to_all x4, blocking collectives, swap(): return lax.all_to_all(blocks, axes, split_axis=0, concat_axis=0, tiled=True)  65.4 us
    pallas_call x10, Pallas kernels, call(): pl.pallas_call(kernel, out_shape=shapes, in_specs=[pl.BlockSpec(memory_sp...  9.41 us
  transfers between devices with their start and end apart: 3, of which 2 were waited for; matrix products, arithmetic and copies ran while one was open for 0% of the time, Pallas kernels for 4%

profile of v3, /device:TPU:0, one launch (start us, length us, event | category | flops | bytes accessed | tf_op | source)
XLA Modules:
  0.0 77.4 jit_solution(17944218436822403104)
XLA Ops:
  0.0 2.6 %shard_map.100 = (bf16[32,24,128]{2,1,0:T(8,128)(2,1)S(1)}, bf16[128,16384]{1,0:T(8,128)(2,1)S(1)}, bf16[16,128]{1,0:T(8,128)(2,1)S(1)}) custom-call(s32[16]{0:T(128)} %lengths_hbm.1, bf16[16,32,128]{2,1,0:T(8,128)(2,1)} %q_hbm.1, bf16[16,128,128]{2,1,0:T(8,128)(2,1)} %bitcast.11, bf16[16,128,128]{2,1,0:T(8,128)(2,1)} %bitcast.12, ...), custom_call_target="tpu_custom_call" | custom-call | bytes 1048576 | tf_op jit(solution)/shard_map/pallas_call | solution.py:28
  2.6 15.6 %all_to_all.20.came_ref = bf16[32,24,128]{2,1,0:T(8,128)(2,1)S(1)} all-to-all(bf16[32,24,128]{2,1,0:T(8,128)(2,1)S(1)} %get-tuple-element.17), channel_id=1, replica_groups=mesh['x'=4,'y'=4,'c'=2,'z'=4] {'x','y','c'}, dimensions={0} | all-to-all | bytes 393216 | tf_op jit(solution)/shard_map/all_to_all | solution.py:302
  18.2 0.0 slice-start
  18.2 0.0 slice-start.2
  18.2 0.0 slice-start.1
  18.2 0.0 slice-start.3
  18.2 0.6 shard_map.101
  18.8 0.0 copy-start
  18.8 0.3 collective-permute-start
  19.2 0.4 shard_map.102.own_ref
  19.5 0.9 %collective-permute-done.came_ref = bf16[64,16,128]{2,1,0:T(8,128)(2,1)S(1)} collective-permute-done((bf16[64,16,128]{2,1,0:T(8,128)(2,1)S(1)}, bf16[64,16,128]{2,1,0:T(8,128)(2,1)S(1)}, u32[]{:S(2)}, u32[]{:S(2)}) %collective-permute-start) | collective-permute-done | bytes 262176 | tf_op jit(solution)/shard_map/ppermute | solution.py:306
  20.5 18.6 %all_to_all.21.came_ref = bf16[64,16,128]{2,1,0:T(8,128)(2,1)S(1)} all-to-all(bf16[64,16,128]{2,1,0:T(8,128)(2,1)S(1)} %shard_map.103), channel_id=1, replica_groups=mesh['x'=4,'y'=4,'c'=2,'z'=4] {'x','y','z'}, dimensions={0} | all-to-all | bytes 524288 | tf_op jit(solution)/shard_map/all_to_all | solution.py:302
  39.1 0.0 slice-start.4
  39.1 0.1 shard_map.104
  39.2 15.5 %all_to_all.22.whole_ref = bf16[64,16,128]{2,1,0:T(8,128)(2,1)S(1)} all-to-all(bf16[64,16,128]{2,1,0:T(8,128)(2,1)S(1)} %get-tuple-element.23), channel_id=1, replica_groups=mesh['x'=4,'y'=4,'c'=2,'z'=4] {'x','y','z'}, dimensions={0} | all-to-all | bytes 524288 | tf_op jit(solution)/shard_map/all_to_all | solution.py:302
  54.7 0.0 collective-permute-start.1
  54.7 0.0 copy-done
  54.7 0.0 slice-done
  54.7 0.0 slice-done.2
  54.7 0.0 slice-done.1
  54.7 0.0 slice-done.3
  54.8 0.0 slice-start.5
  54.8 1.9 %shard_map.105 = (f32[208,16]{1,0:T(8,128)S(1)}, f32[208,16]{1,0:T(8,128)S(1)}, f32[16,128]{1,0:T(8,128)S(1)}) custom-call(bf16[64,16,128]{2,1,0:T(8,128)(2,1)S(1)} %all_to_all.22.whole_ref, f32[128,128]{1,0:T(8,128)S(1)} %bitcast_convert_fusion.gain_ref, bf16[208,16384]{1,0:T(8,128)(2,1)S(1)} %bitcast.6, bf16[208,16384]{1,0:T(8,128)(2,1)S(1)} %bitcast.8), custom_call_target="tpu_custom_call" | custom-call | flops 1000000000 | bytes 1048576 | tf_op jit(solution)/shard_map/pallas_call | solution.py:28
  56.7 0.0 collective-permute-done.1.whole_ref
  56.7 0.0 slice-done.4
  56.7 0.0 slice-done.5
  56.7 2.5 %shard_map.106 = (bf16[64,16,128]{2,1,0:T(8,128)(2,1)S(1)}, bf16[16,208]{1,0:T(8,128)(2,1)S(1)}) custom-call(bf16[64,16,128]{2,1,0:T(8,128)(2,1)S(1)} %collective-permute-done.1.whole_ref, f32[128,128]{1,0:T(8,128)S(1)} %bitcast_convert_fusion.gain_ref, bf16[208,16384]{1,0:T(8,128)(2,1)S(1)} %bitcast.6, bf16[208,16384]{1,0:T(8,128)(2,1)S(1)} %bitcast.8, ...), custom_call_target="tpu_custom_call" | custom-call | bytes 1048576 | tf_op jit(solution)/shard_map/pallas_call | solution.py:28
  59.2 0.6 collective-permute-start.2
  59.8 0.5 shard_map.107.own_ref
  60.3 0.6 collective-permute-done.2.came_ref
  61.0 15.8 %all_to_all.23.came_ref = bf16[64,16,128]{2,1,0:T(8,128)(2,1)S(1)} all-to-all(bf16[64,16,128]{2,1,0:T(8,128)(2,1)S(1)} %shard_map.108), channel_id=1, replica_groups=mesh['x'=4,'y'=4,'c'=2,'z'=4] {'x','y','z'}, dimensions={0} | all-to-all | bytes 524288 | tf_op jit(solution)/shard_map/all_to_all | solution.py:302
  76.7 0.7 shard_map.109
  (6 shorter events, 0.1 us)
Async XLA Ops:
  18.2 36.5 %slice-start = ((s8[6815744]{0:T(1024)(128)(4,1)}), s8[4194304]{0:T(1024)(128)(4,1)S(1)}, s32[]{:S(2)}) async-start(s8[6815744]{0:T(1024)(128)(4,1)} %bitcast.5), calls=%async_computation.4 | async-start | bytes 8388608
  18.2 36.5 %slice-start.2 = ((s8[6815744]{0:T(1024)(128)(4,1)}), s8[4194304]{0:T(1024)(128)(4,1)S(1)}, s32[]{:S(2)}) async-start(s8[6815744]{0:T(1024)(128)(4,1)} %bitcast.7), calls=%async_computation.6 | async-start | bytes 8388608
  18.2 36.5 %slice-start.1 = ((s8[6815744]{0:T(1024)(128)(4,1)}), s8[2621440]{0:T(1024)(128)(4,1)S(1)}, s32[]{:S(2)}) async-start(s8[6815744]{0:T(1024)(128)(4,1)} %bitcast.5), calls=%async_computation.5 | async-start | bytes 5242880
  18.2 36.5 %slice-start.3 = ((s8[6815744]{0:T(1024)(128)(4,1)}), s8[2621440]{0:T(1024)(128)(4,1)S(1)}, s32[]{:S(2)}) async-start(s8[6815744]{0:T(1024)(128)(4,1)} %bitcast.7), calls=%async_computation.7 | async-start | bytes 5242880
  18.8 35.9 %copy-start = (bf16[16384]{0:T(1024)(128)(2,1)S(1)}, bf16[16384]{0:T(1024)(128)(2,1)}, u32[]{:S(2)}) copy-start(bf16[16384]{0:T(1024)(128)(2,1)} %param.16) | copy-start | bytes 98308
  18.8 1.6 %collective-permute-start = (bf16[64,16,128]{2,1,0:T(8,128)(2,1)S(1)}, bf16[64,16,128]{2,1,0:T(8,128)(2,1)S(1)}, u32[]{:S(2)}, u32[]{:S(2)}) collective-permute-start(bf16[64,16,128]{2,1,0:T(8,128)(2,1)S(1)} %get-tuple-element.20), channel_id=1, source_target_pairs={{0,4},{4,0},{1,5},{5,1},{2,6},{6,2},{3,7},{7,3},{8,12},{12,8},{9,1... | collective-permute-start | bytes 786440 | tf_op jit(solution)/shard_map/ppermute | solution.py:306
  39.1 17.6 %slice-start.4 = ((s8[6815744]{0:T(1024)(128)(4,1)}), s8[4194304]{0:T(1024)(128)(4,1)S(1)}, s32[]{:S(2)}) async-start(s8[6815744]{0:T(1024)(128)(4,1)} %bitcast.9), calls=%async_computation.8 | async-start | bytes 8388608
  54.7 2.0 %collective-permute-start.1 = (bf16[64,16,128]{2,1,0:T(8,128)(2,1)S(1)}, bf16[64,16,128]{2,1,0:T(8,128)(2,1)S(1)}, u32[]{:S(2)}, u32[]{:S(2)}) collective-permute-start(bf16[64,16,128]{2,1,0:T(8,128)(2,1)S(1)} %all_to_all.22.whole_ref), channel_id=1, source_target_pairs={{0,4},{4,0},{1,5},{5,1},{2,6},{6,2},{3,7},{7,3},{8,12},{12,8},{9,1... | collective-permute-start | bytes 786440 | tf_op jit(solution)/shard_map/ppermute | solution.py:306
  54.8 1.9 %slice-start.5 = ((s8[6815744]{0:T(1024)(128)(4,1)}), s8[2621440]{0:T(1024)(128)(4,1)S(1)}, s32[]{:S(2)}) async-start(s8[6815744]{0:T(1024)(128)(4,1)} %bitcast.9), calls=%async_computation.9 | async-start | bytes 5242880
  59.2 1.7 %collective-permute-start.2 = (bf16[64,16,128]{2,1,0:T(8,128)(2,1)S(1)}, bf16[64,16,128]{2,1,0:T(8,128)(2,1)S(1)}, u32[]{:S(2)}, u32[]{:S(2)}) collective-permute-start(bf16[64,16,128]{2,1,0:T(8,128)(2,1)S(1)} %get-tuple-element.28), channel_id=1, source_target_pairs={{0,4},{4,0},{1,5},{5,1},{2,6},{6,2},{3,7},{7,3},{8,12},{12,8},{9,1... | collective-permute-start | bytes 786440 | tf_op jit(solution)/shard_map/ppermute | solution.py:306

commit v4 on v3

--- a/solution.py
+++ b/solution.py
@@ -42,23 +42,20 @@
     q_hbm,
     k_hbm,
     v_hbm,
-    weight_hbm,
     residual_hbm,
-    message_ref,
-    weight_ref,
+    weights_ref,
+    stats_ref,
+    v_ref,
     residual_ref,
     lengths_ref,
     q_ref,
     k_ref,
-    v_ref,
-    held,
     sems,
 ):
     rows, heads, width = q_ref.shape
     slots = k_ref.shape[1]
     span = slots // groups
     size = heads // groups
-    height = message_ref.shape[1]
     columns = pl.ds(pl.multiple_of(flat_index(ALL) * LANES, LANES), LANES)
     loads = [
         pltpu.make_async_copy(source, target, sems.at[i])
@@ -68,7 +65,6 @@
                 (k_hbm, k_ref),
                 (lengths_hbm, lengths_ref),
                 (v_hbm, v_ref),
-                (weight_hbm, weight_ref),
                 (residual_hbm.at[:, columns], residual_ref),
             )
         )
@@ -88,59 +84,71 @@
         lax.dot_general(q_ref[b], k_ref[b], LAST, preferred_element_type=jnp.float32) * width ** (-0.5)
         for b in range(rows)
     ]
-    weights, packed = [], []
     for b in range(rows):
         live = position < lengths_ref[b]
         masked = jnp.where(live, scores[b], -1e30)
         point = jnp.max(masked, axis=1, keepdims=True).astype(jnp.bfloat16).astype(jnp.float32)
         weight = jnp.where(live, jnp.exp(masked - point), 0.0)
-        weights.append(weight.astype(jnp.bfloat16))
-        packed.append((point, jnp.sum(weight, axis=1, keepdims=True)))
-    loads[3].wait()
-    outs = [jnp.dot(weights[b], v_ref[b], preferred_element_type=jnp.float32) for b in range(rows)]
-    for b in range(rows):
-        held[pl.ds(b, heads, stride=height), :] = outs[b]
-    for b in range(rows // 2):
-        (point, total), (later_point, later_total) = packed[b], packed[b + rows // 2]
-        stats = jnp.where(
-            lane < half,
-            jnp.where(lane < half // 2, point, total),
-            jnp.where(lane < half + half // 2, later_point, later_total),
-        )
-        held[pl.ds(rows + b, heads, stride=height), :] = stats
-    for h in range(heads):
-        message_ref[h] = held[h * height : (h + 1) * height, :].astype(jnp.bfloat16)
-    loads[4].wait()
-    loads[5].wait()
-
-
-def attention(lengths, queries, k_cache, v_cache, weight, residual):
+        weights_ref[b] = weight.astype(jnp.bfloat16)
+        stats_ref[b] = jnp.where(lane < half // 2, point, jnp.sum(weight, axis=1, keepdims=True))
+    for load in loads[3:]:
+        load.wait()
+
+
+def attention(lengths, queries, k_cache, v_cache, residual):
     rows, heads, width = queries.shape
     span, groups = k_cache.shape[1:3]
-    height = rows + rows // 2
     cache = (rows, span * groups, width)
     return call(
         functools.partial(attention_kernel, groups),
         [
-            ((heads, height, width), jnp.bfloat16),
-            (weight.shape, jnp.bfloat16),
+            ((rows, heads, span * groups), jnp.bfloat16),
+            (queries.shape, jnp.float32),
+            (cache, jnp.bfloat16),
             ((rows, LANES), jnp.bfloat16),
         ],
         [
             pltpu.with_memory_space_constraint(a, pltpu.HBM)
-            for a in (lengths, queries, k_cache.reshape(cache), v_cache.reshape(cache), weight, residual)
+            for a in (lengths, queries, k_cache.reshape(cache), v_cache.reshape(cache), residual)
         ],
-        [pltpu.HBM] * 6,
+        [pltpu.HBM] * 5,
         [
             pltpu.SMEM(lengths.shape, jnp.int32),
             pltpu.VMEM(queries.shape, jnp.bfloat16),
             pltpu.VMEM(cache, jnp.bfloat16),
-            pltpu.VMEM(cache, jnp.bfloat16),
-            pltpu.VMEM((heads * height, width), jnp.float32),
-            pltpu.SemaphoreType.DMA((6,)),
+            pltpu.SemaphoreType.DMA((5,)),
         ],
         limit=12 * MIB,
     )
+
+
+def message_kernel(weights_ref, stats_ref, v_ref, message_ref, held):
+    rows, heads, _ = weights_ref.shape
+    _, height, width = message_ref.shape
+    half = width // 2
+    lane = lax.broadcasted_iota(jnp.int32, (heads, width), 1)
+    outs = [jnp.dot(weights_ref[b], v_ref[b], preferred_element_type=jnp.float32) for b in range(rows)]
+    for b in range(rows):
+        held[pl.ds(b, heads, stride=height), :] = outs[b]
+    for b in range(rows // 2):
+        later = pltpu.roll(stats_ref[b + rows // 2], half, 1)
+        held[pl.ds(rows + b, heads, stride=height), :] = jnp.where(lane < half, stats_ref[b], later)
+    for h in range(heads):
+        message_ref[h] = held[h * height : (h + 1) * height, :].astype(jnp.bfloat16)
+
+
+def message_of(weights, stats, values):
+    rows, heads, width = stats.shape
+    height = rows + rows // 2
+    return call(
+        message_kernel,
+        [((heads, height, width), jnp.bfloat16)],
+        [weights, stats, values],
+        [pltpu.VMEM] * 3,
+        [pltpu.VMEM((heads * height, width), jnp.float32)],
+        limit=8 * MIB,
+        flops=10**10,
+    )[0]
 
 
 def columns_of(piece, side, run):
@@ -311,9 +319,10 @@
 ):
     rows = queries.shape[0]
     gain = norm_gain.astype(jnp.float32).reshape(-1, LANES)
-    message, weight, residual = attention(lengths, queries, k_cache, v_cache, out_weight, residual_in)
-    sent, attended = merge_and_project(swap(message, KV), weight, rows)
-    partial = add(own_half(attended, weight), other(sent))
+    weights, stats, values, residual = attention(lengths, queries, k_cache, v_cache, residual_in)
+    came = swap(message_of(weights, stats, values), KV)
+    sent, attended = merge_and_project(came, out_weight, rows)
+    partial = add(own_half(attended, out_weight), other(sent))
     stream, copies = stream_sum(swap(partial, CHIPS), residual)
     whole = swap(copies, CHIPS)
     sums = first_half(whole, gain, gate_weight, up_weight)

time: 77.6 us -> 77.1 us (level)
    pallas_call x10 -> x11, Pallas kernels: 9.41 us -> 8.76 us  [call(): pl.pallas_call(kernel, out_shape=shapes, in_specs=[pl.BlockSpec(memory_sp...]
where the time goes in v4:
time: 77.1 us; the launch traced here: 76.8 us
  blocking collectives  65.4 us (85%)
  Pallas kernels  8.76 us (11%)
  waiting for transfers between devices  1.52 us (2%)
  starting transfers between devices  0.9 us (1%)
    all_to_all x4, blocking collectives, swap(): return lax.all_to_all(blocks, axes, split_axis=0, concat_axis=0, tiled=True)  65.4 us
    pallas_call x11, Pallas kernels, call(): pl.pallas_call(kernel, out_shape=shapes, in_specs=[pl.BlockSpec(memory_sp...  8.76 us
  transfers between devices with their start and end apart: 3, of which 2 were waited for; matrix products, arithmetic and copies ran while one was open for 0% of the time, Pallas kernels for 4%

profile of v4, /device:TPU:0, one launch (start us, length us, event | category | flops | bytes accessed | tf_op | source)
XLA Modules:
  0.0 76.8 jit_solution(15959186391328838584)
XLA Ops:
  0.0 1.7 %shard_map.100 = (bf16[16,32,128]{2,1,0:T(8,128)(2,1)S(1)}, f32[16,32,128]{2,1,0:T(8,128)S(1)}, bf16[16,128,128]{2,1,0:T(8,128)(2,1)S(1)}, bf16[16,128]{1,0:T(8,128)(2,1)S(1)}) custom-call(s32[16]{0:T(128)} %lengths_hbm.1, bf16[16,32,128]{2,1,0:T(8,128)(2,1)} %q_hbm.1, bf16[16,128,128]{2,1,0:T(8,128)(2,1)} %bitcast.11, bf16[16,128,128]{2,1,0:T(8,128)(2,1)} %bitcast.12, ...), custom_call_target="tpu_custom_call" | custom-call | bytes 1048576 | tf_op jit(solution)/shard_map/pallas_call | solution.py:28
  1.7 0.0 copy-start
  1.7 0.3 shard_map.101
  2.0 0.0 slice-start
  2.0 0.0 slice-start.2
  2.0 15.8 %all_to_all.20.came_ref = bf16[32,24,128]{2,1,0:T(8,128)(2,1)S(1)} all-to-all(bf16[32,24,128]{2,1,0:T(8,128)(2,1)S(1)} %shard_map.101), channel_id=1, replica_groups=mesh['x'=4,'y'=4,'c'=2,'z'=4] {'x','y','c'}, dimensions={0} | all-to-all | bytes 393216 | tf_op jit(solution)/shard_map/all_to_all | solution.py:310
  17.9 0.0 copy-done
  17.9 0.6 shard_map.102
  18.5 0.0 copy-start.1
  18.5 0.3 collective-permute-start
  18.8 0.4 shard_map.103.own_ref
  19.2 0.9 %collective-permute-done.came_ref = bf16[64,16,128]{2,1,0:T(8,128)(2,1)S(1)} collective-permute-done((bf16[64,16,128]{2,1,0:T(8,128)(2,1)S(1)}, bf16[64,16,128]{2,1,0:T(8,128)(2,1)S(1)}, u32[]{:S(2)}, u32[]{:S(2)}) %collective-permute-start) | collective-permute-done | bytes 262176 | tf_op jit(solution)/shard_map/ppermute | solution.py:314
  20.2 0.0 slice-start.4
  20.2 18.6 %all_to_all.21.came_ref = bf16[64,16,128]{2,1,0:T(8,128)(2,1)S(1)} all-to-all(bf16[64,16,128]{2,1,0:T(8,128)(2,1)S(1)} %shard_map.104), channel_id=1, replica_groups=mesh['x'=4,'y'=4,'c'=2,'z'=4] {'x','y','z'}, dimensions={0} | all-to-all | bytes 524288 | tf_op jit(solution)/shard_map/all_to_all | solution.py:310
  38.8 0.1 shard_map.105
  38.9 15.2 %all_to_all.22.whole_ref = bf16[64,16,128]{2,1,0:T(8,128)(2,1)S(1)} all-to-all(bf16[64,16,128]{2,1,0:T(8,128)(2,1)S(1)} %get-tuple-element.25), channel_id=1, replica_groups=mesh['x'=4,'y'=4,'c'=2,'z'=4] {'x','y','z'}, dimensions={0} | all-to-all | bytes 524288 | tf_op jit(solution)/shard_map/all_to_all | solution.py:310
  54.1 0.0 collective-permute-start.1
  54.1 0.0 copy-done.1
  54.1 0.0 slice-done
  54.1 0.0 slice-done.2
  54.1 0.0 slice-done.1
  54.1 0.0 slice-done.3
  54.2 0.0 slice-start.5
  54.2 1.9 %shard_map.106 = (f32[208,16]{1,0:T(8,128)S(1)}, f32[208,16]{1,0:T(8,128)S(1)}, f32[16,128]{1,0:T(8,128)S(1)}) custom-call(bf16[64,16,128]{2,1,0:T(8,128)(2,1)S(1)} %all_to_all.22.whole_ref, f32[128,128]{1,0:T(8,128)S(1)} %bitcast_convert_fusion.gain_ref, bf16[208,16384]{1,0:T(8,128)(2,1)S(1)} %bitcast.6, bf16[208,16384]{1,0:T(8,128)(2,1)S(1)} %bitcast.8), custom_call_target="tpu_custom_call" | custom-call | flops 1000000000 | bytes 1048576 | tf_op jit(solution)/shard_map/pallas_call | solution.py:28
  56.1 0.0 collective-permute-done.1.whole_ref
  56.1 0.0 slice-done.4
  56.1 2.5 %shard_map.107 = (bf16[64,16,128]{2,1,0:T(8,128)(2,1)S(1)}, bf16[16,208]{1,0:T(8,128)(2,1)S(1)}) custom-call(bf16[64,16,128]{2,1,0:T(8,128)(2,1)S(1)} %collective-permute-done.1.whole_ref, f32[128,128]{1,0:T(8,128)S(1)} %bitcast_convert_fusion.gain_ref, bf16[208,16384]{1,0:T(8,128)(2,1)S(1)} %bitcast.6, bf16[208,16384]{1,0:T(8,128)(2,1)S(1)} %bitcast.8, ...), custom_call_target="tpu_custom_call" | custom-call | bytes 1048576 | tf_op jit(solution)/shard_map/pallas_call | solution.py:28
  58.6 0.6 collective-permute-start.2
  59.2 0.5 shard_map.108.own_ref
  59.7 0.6 collective-permute-done.2.came_ref
  60.4 15.8 %all_to_all.23.came_ref = bf16[64,16,128]{2,1,0:T(8,128)(2,1)S(1)} all-to-all(bf16[64,16,128]{2,1,0:T(8,128)(2,1)S(1)} %shard_map.109), channel_id=1, replica_groups=mesh['x'=4,'y'=4,'c'=2,'z'=4] {'x','y','z'}, dimensions={0} | all-to-all | bytes 524288 | tf_op jit(solution)/shard_map/all_to_all | solution.py:310
  76.1 0.7 shard_map.110
  (9 shorter events, 0.1 us)
Async XLA Ops:
  1.7 16.1 %copy-start = (bf16[128,16384]{1,0:T(8,128)(2,1)S(1)}, bf16[128,16384]{1,0:T(8,128)(2,1)}, u32[]{:S(2)}) copy-start(bf16[128,16384]{1,0:T(8,128)(2,1)} %weight_ref.4) | copy-start | bytes 12582916
  2.0 52.1 %slice-start = ((s8[6815744]{0:T(1024)(128)(4,1)}), s8[4194304]{0:T(1024)(128)(4,1)S(1)}, s32[]{:S(2)}) async-start(s8[6815744]{0:T(1024)(128)(4,1)} %bitcast.5), calls=%async_computation.4 | async-start | bytes 8388608
  2.0 52.1 %slice-start.2 = ((s8[6815744]{0:T(1024)(128)(4,1)}), s8[4194304]{0:T(1024)(128)(4,1)S(1)}, s32[]{:S(2)}) async-start(s8[6815744]{0:T(1024)(128)(4,1)} %bitcast.7), calls=%async_computation.6 | async-start | bytes 8388608
  17.9 36.3 %slice-start.1 = ((s8[6815744]{0:T(1024)(128)(4,1)}), s8[2621440]{0:T(1024)(128)(4,1)S(1)}, s32[]{:S(2)}) async-start(s8[6815744]{0:T(1024)(128)(4,1)} %bitcast.5), calls=%async_computation.5 | async-start | bytes 5242880
  17.9 36.3 %slice-start.3 = ((s8[6815744]{0:T(1024)(128)(4,1)}), s8[2621440]{0:T(1024)(128)(4,1)S(1)}, s32[]{:S(2)}) async-start(s8[6815744]{0:T(1024)(128)(4,1)} %bitcast.7), calls=%async_computation.7 | async-start | bytes 5242880
  18.5 35.6 %copy-start.1 = (bf16[16384]{0:T(1024)(128)(2,1)S(1)}, bf16[16384]{0:T(1024)(128)(2,1)}, u32[]{:S(2)}) copy-start(bf16[16384]{0:T(1024)(128)(2,1)} %param.16) | copy-start | bytes 98308
  18.5 1.6 %collective-permute-start = (bf16[64,16,128]{2,1,0:T(8,128)(2,1)S(1)}, bf16[64,16,128]{2,1,0:T(8,128)(2,1)S(1)}, u32[]{:S(2)}, u32[]{:S(2)}) collective-permute-start(bf16[64,16,128]{2,1,0:T(8,128)(2,1)S(1)} %get-tuple-element.22), channel_id=1, source_target_pairs={{0,4},{4,0},{1,5},{5,1},{2,6},{6,2},{3,7},{7,3},{8,12},{12,8},{9,1... | collective-permute-start | bytes 786440 | tf_op jit(solution)/shard_map/ppermute | solution.py:314
  20.2 35.9 %slice-start.4 = ((s8[6815744]{0:T(1024)(128)(4,1)}), s8[4194304]{0:T(1024)(128)(4,1)S(1)}, s32[]{:S(2)}) async-start(s8[6815744]{0:T(1024)(128)(4,1)} %bitcast.9), calls=%async_computation.8 | async-start | bytes 8388608
  54.1 2.0 %collective-permute-start.1 = (bf16[64,16,128]{2,1,0:T(8,128)(2,1)S(1)}, bf16[64,16,128]{2,1,0:T(8,128)(2,1)S(1)}, u32[]{:S(2)}, u32[]{:S(2)}) collective-permute-start(bf16[64,16,128]{2,1,0:T(8,128)(2,1)S(1)} %all_to_all.22.whole_ref), channel_id=1, source_target_pairs={{0,4},{4,0},{1,5},{5,1},{2,6},{6,2},{3,7},{7,3},{8,12},{12,8},{9,1... | collective-permute-start | bytes 786440 | tf_op jit(solution)/shard_map/ppermute | solution.py:314
  54.2 1.9 %slice-start.5 = ((s8[6815744]{0:T(1024)(128)(4,1)}), s8[2621440]{0:T(1024)(128)(4,1)S(1)}, s32[]{:S(2)}) async-start(s8[6815744]{0:T(1024)(128)(4,1)} %bitcast.9), calls=%async_computation.9 | async-start | bytes 5242880
  58.6 1.7 %collective-permute-start.2 = (bf16[64,16,128]{2,1,0:T(8,128)(2,1)S(1)}, bf16[64,16,128]{2,1,0:T(8,128)(2,1)S(1)}, u32[]{:S(2)}, u32[]{:S(2)}) collective-permute-start(bf16[64,16,128]{2,1,0:T(8,128)(2,1)S(1)} %get-tuple-element.30), channel_id=1, source_target_pairs={{0,4},{4,0},{1,5},{5,1},{2,6},{6,2},{3,7},{7,3},{8,12},{12,8},{9,1... | collective-permute-start | bytes 786440 | tf_op jit(solution)/shard_map/ppermute | solution.py:314

commit v5 on v4

--- a/solution.py
+++ b/solution.py
@@ -7,9 +7,10 @@
 from jax.experimental.pallas import tpu as pltpu
 from jax.sharding import Mesh, PartitionSpec as P
 
-KV = ("x", "y", "c")
-ALL = ("x", "y", "c", "z")
-CHIPS = ("x", "y", "z")
+KV = ("far", "x", "y", "c")
+ALL = ("far", "x", "y", "c", "z")
+CHIPS = ("far", "x", "y", "z")
+NEAR = ("x", "y", "z")
 LANES = 128
 MIB = 2**20
 LAST = (((1,), (1,)), ((), ()))
@@ -56,7 +57,9 @@
     slots = k_ref.shape[1]
     span = slots // groups
     size = heads // groups
-    columns = pl.ds(pl.multiple_of(flat_index(ALL) * LANES, LANES), LANES)
+    near = flat_index(("x", "y", "c", "z"))
+    distance = lax.axis_size(("x", "y", "c", "z"))
+    starts = [pl.multiple_of((near + i * distance) * LANES, LANES) for i in range(lax.axis_size("far"))]
     loads = [
         pltpu.make_async_copy(source, target, sems.at[i])
         for i, (source, target) in enumerate(
@@ -65,7 +68,8 @@
                 (k_hbm, k_ref),
                 (lengths_hbm, lengths_ref),
                 (v_hbm, v_ref),
-                (residual_hbm.at[:, columns], residual_ref),
+                (residual_hbm.at[:, pl.ds(starts[0], LANES)], residual_ref.at[0]),
+                (residual_hbm.at[:, pl.ds(starts[1], LANES)], residual_ref.at[1]),
             )
         )
     ]
@@ -105,7 +109,7 @@
             ((rows, heads, span * groups), jnp.bfloat16),
             (queries.shape, jnp.float32),
             (cache, jnp.bfloat16),
-            ((rows, LANES), jnp.bfloat16),
+            ((2, rows, LANES), jnp.bfloat16),
         ],
         [
             pltpu.with_memory_space_constraint(a, pltpu.HBM)
@@ -116,7 +120,7 @@
             pltpu.SMEM(lengths.shape, jnp.int32),
             pltpu.VMEM(queries.shape, jnp.bfloat16),
             pltpu.VMEM(cache, jnp.bfloat16),
-            pltpu.SemaphoreType.DMA((5,)),
+            pltpu.SemaphoreType.DMA((6,)),
         ],
         limit=12 * MIB,
     )
@@ -159,13 +163,17 @@
     return 1 - lax.axis_index("c")
 
 
-def half_product(left, weight_ref, side, out_ref):
+def half_product(left, weight_ref, side, out_ref, paired):
     per = lax.axis_size("z")
     run = per * LANES
-    for piece in range(out_ref.shape[0] // per):
+    places = out_ref.shape[0] // per
+    halves = lax.axis_size("far")
+    for piece in range(places):
         product = jnp.dot(left, weight_ref[:, columns_of(piece, side, run)], preferred_element_type=jnp.float32)
+        half, near = divmod(piece, places // halves)
         for j in range(per):
-            out_ref[piece * per + j] = product[:, j * LANES : (j + 1) * LANES].astype(out_ref.dtype)
+            at = (near * per + j) * halves + half if paired else piece * per + j
+            out_ref[at] = product[:, j * LANES : (j + 1) * LANES].astype(out_ref.dtype)
 
 
 def merge_kernel(rows, came_ref, weight_ref, sent_ref, attended_ref):
@@ -181,7 +189,7 @@
     out = jnp.sum(scale * came_ref[:, :rows, :].astype(jnp.float32), axis=0)
     attended = (out / jnp.sum(scale * total, axis=0)).astype(jnp.bfloat16)
     attended_ref[...] = attended
-    half_product(attended, weight_ref, other_core(), sent_ref)
+    half_product(attended, weight_ref, other_core(), sent_ref, True)
 
 
 def merge_and_project(came, weight, rows):
@@ -196,14 +204,14 @@
     )
 
 
-def own_kernel(left_ref, weight_ref, out_ref):
-    half_product(left_ref[...], weight_ref, lax.axis_index("c"), out_ref)
-
-
-def own_half(left, weight):
+def own_kernel(paired, left_ref, weight_ref, out_ref):
+    half_product(left_ref[...], weight_ref, lax.axis_index("c"), out_ref, paired)
+
+
+def own_half(left, weight, paired):
     chips = weight.shape[1] // LANES // 2
     return call(
-        own_kernel,
+        functools.partial(own_kernel, paired),
         [((chips, left.shape[0], LANES), jnp.float32)],
         [left, weight],
         [pltpu.VMEM] * 2,
@@ -220,30 +228,37 @@
     return call(add_kernel, [(came.shape, jnp.bfloat16)], [own, came], [pltpu.VMEM] * 2)[0]
 
 
-def stream_kernel(came_ref, residual_ref, stream_ref, sent_ref):
+def stream_kernel(came_ref, residual_ref, sent_ref):
     total = jnp.sum(came_ref[...].astype(jnp.float32), axis=0)
-    stream = total + residual_ref[...].astype(jnp.float32)
-    stream_ref[...] = stream
-    sent_ref[...] = jnp.broadcast_to(stream.astype(jnp.bfloat16)[None], sent_ref.shape)
+    residual = residual_ref[...].astype(jnp.float32)
+    total += jnp.where(lax.axis_index("far") == 0, residual, 0.0)
+    sent_ref[...] = jnp.broadcast_to(total.astype(jnp.bfloat16)[None], sent_ref.shape)
 
 
 def stream_sum(came, residual):
-    shape = came.shape
+    chips = lax.axis_size(CHIPS)
     return call(
         stream_kernel,
-        [(shape[1:], jnp.float32), (shape, jnp.bfloat16)],
+        [((chips, *residual.shape), jnp.bfloat16)],
         [came, residual],
         [pltpu.VMEM] * 2,
-    )
+    )[0]
+
+
+def stream_block(whole_ref, near, half):
+    chips = whole_ref.shape[0] // lax.axis_size("far")
+    return whole_ref[near, half].astype(jnp.float32) + whole_ref[chips + near, half].astype(jnp.float32)
 
 
 def gate_up(side, whole_ref, gain_ref, gate_ref, up_ref, gate, up, square):
     per = lax.axis_size("z")
     run = per * LANES
-    for piece in range(whole_ref.shape[0] // per):
+    places = whole_ref.shape[0] // per
+    for piece in range(places):
+        half, near = divmod(piece, places // lax.axis_size("far"))
         parts = []
         for j in range(per):
-            part = whole_ref[piece * per + j].astype(jnp.float32)
+            part = stream_block(whole_ref, near * per + j, half)
             square += part * part
             gain = gain_ref[pl.ds((2 * piece + side) * per + j, 1), :]
             parts.append((part * gain).astype(jnp.bfloat16))
@@ -254,18 +269,19 @@
     return gate, up, square
 
 
-def first_kernel(whole_ref, gain_ref, gate_ref, up_ref, gate_out, up_out, square_out):
+def first_kernel(whole_ref, gain_ref, gate_ref, up_ref, gate_out, up_out, square_out, stream_out):
     zeros = jnp.zeros(gate_out.shape, jnp.float32)
     gate_out[...], up_out[...], square_out[...] = gate_up(
         lax.axis_index("c"), whole_ref, gain_ref, gate_ref, up_ref, zeros, zeros, jnp.zeros(square_out.shape, jnp.float32)
     )
+    stream_out[...] = stream_block(whole_ref, flat_index(NEAR), lax.axis_index("far"))
 
 
 def first_half(whole, gain, gate, up):
-    rows, units = whole.shape[1], gate.shape[0]
+    rows, units = whole.shape[2], gate.shape[0]
     return call(
         first_kernel,
-        [((units, rows), jnp.float32), ((units, rows), jnp.float32), ((rows, LANES), jnp.float32)],
+        [((units, rows), jnp.float32)] * 2 + [((rows, LANES), jnp.float32)] * 2,
         [whole, gain, gate, up],
         [pltpu.VMEM] * 4,
         limit=24 * MIB,
@@ -284,13 +300,13 @@
     gate = gate * factor
     hidden = (gate / (1.0 + jnp.exp(-gate)) * (up * factor)).T.astype(jnp.bfloat16)
     hidden_ref[...] = hidden
-    half_product(hidden, down_ref, other_core(), sent_ref)
+    half_product(hidden, down_ref, other_core(), sent_ref, False)
 
 
 def second_half(whole, gain, gate, up, down, sums):
     return call(
         second_kernel,
-        [(whole.shape, jnp.bfloat16), ((whole.shape[1], gate.shape[0]), jnp.bfloat16)],
+        [((whole.shape[0], *whole.shape[2:]), jnp.bfloat16), ((whole.shape[2], gate.shape[0]), jnp.bfloat16)],
         [whole, gain, gate, up, down, *sums],
         [pltpu.VMEM] * 8,
         limit=30 * MIB,
@@ -322,17 +338,18 @@
     weights, stats, values, residual = attention(lengths, queries, k_cache, v_cache, residual_in)
     came = swap(message_of(weights, stats, values), KV)
     sent, attended = merge_and_project(came, out_weight, rows)
-    partial = add(own_half(attended, out_weight), other(sent))
-    stream, copies = stream_sum(swap(partial, CHIPS), residual)
-    whole = swap(copies, CHIPS)
-    sums = first_half(whole, gain, gate_weight, up_weight)
+    partial = add(own_half(attended, out_weight, True), other(sent))
+    near = lax.axis_size(NEAR)
+    partial = swap(partial.reshape(near, -1, rows, LANES), NEAR)
+    whole = swap(stream_sum(partial, residual), CHIPS)
+    *sums, stream = first_half(whole, gain, gate_weight, up_weight)
     sent, hidden = second_half(other(whole), gain, gate_weight, up_weight, down_weight, sums)
-    partial = add(own_half(hidden, down_weight), other(sent))
+    partial = add(own_half(hidden, down_weight, False), other(sent))
     return final_sum(stream, swap(partial, CHIPS))
 
 
 def solution(mesh):
-    fine = Mesh(mesh.devices.reshape(4, 4, 2, 4), ALL)
+    fine = Mesh(mesh.devices.reshape(2, 2, 4, 2, 4), ALL)
     placed = (
         P(None, "z", None),
         P(None, KV, "z", None),

time: 77.1 us -> 76.7 us (level)
  no operation moved by 1% of the time
where the time goes in v5:
time: 76.7 us; the launch traced here: 76.5 us
  blocking collectives  65.1 us (85%)
  Pallas kernels  8.78 us (11%)
  waiting for transfers between devices  1.52 us (2%)
  starting transfers between devices  0.9 us (1%)
    all_to_all x4, blocking collectives, swap(): return lax.all_to_all(blocks, axes, split_axis=0, concat_axis=0, tiled=True)  65.1 us
    pallas_call x11, Pallas kernels, call(): pl.pallas_call(kernel, out_shape=shapes, in_specs=[pl.BlockSpec(memory_sp...  8.78 us
  transfers between devices with their start and end apart: 3, of which 2 were waited for; matrix products, arithmetic and copies ran while one was open for 0% of the time, Pallas kernels for 4%

profile of v5, /device:TPU:0, one launch (start us, length us, event | category | flops | bytes accessed | tf_op | source)
XLA Modules:
  0.0 76.5 jit_solution(2540230192167267741)
XLA Ops:
  0.0 1.7 %shard_map.100 = (bf16[16,32,128]{2,1,0:T(8,128)(2,1)S(1)}, f32[16,32,128]{2,1,0:T(8,128)S(1)}, bf16[16,128,128]{2,1,0:T(8,128)(2,1)S(1)}, bf16[2,16,128]{2,1,0:T(8,128)(2,1)S(1)}) custom-call(s32[16]{0:T(128)} %lengths_hbm.1, bf16[16,32,128]{2,1,0:T(8,128)(2,1)} %q_hbm.1, bf16[16,128,128]{2,1,0:T(8,128)(2,1)} %bitcast.13, bf16[16,128,128]{2,1,0:T(8,128)(2,1)} %bitcast.14, ...), custom_call_target="tpu_custom_call" | custom-call | bytes 1048576 | tf_op jit(solution)/shard_map/pallas_call | solution.py:29
  1.7 0.0 copy-start
  1.8 0.3 shard_map.101
  2.0 0.0 slice-start
  2.0 0.0 slice-start.2
  2.1 15.8 %all_to_all.20.came_ref = bf16[32,24,128]{2,1,0:T(8,128)(2,1)S(1)} all-to-all(bf16[32,24,128]{2,1,0:T(8,128)(2,1)S(1)} %shard_map.101), channel_id=1, replica_groups=mesh['far'=2,'x'=2,'y'=4,'c'=2,'z'=4] {'far','x','y','c'}, dimensions={0} | all-to-all | bytes 393216 | tf_op jit(solution)/shard_map/all_to_all | solution.py:326
  17.9 0.0 copy-done
  17.9 0.6 shard_map.102
  18.5 0.0 copy-start.1
  18.5 0.3 collective-permute-start
  18.8 0.4 shard_map.103.own_ref
  19.2 0.9 %collective-permute-done.came_ref = bf16[64,16,128]{2,1,0:T(8,128)(2,1)S(1)} collective-permute-done((bf16[64,16,128]{2,1,0:T(8,128)(2,1)S(1)}, bf16[64,16,128]{2,1,0:T(8,128)(2,1)S(1)}, u32[]{:S(2)}, u32[]{:S(2)}) %collective-permute-start) | collective-permute-done | bytes 262176 | tf_op jit(solution)/shard_map/ppermute | solution.py:330
  20.1 0.1 shard_map.104
  20.2 15.8 %all_to_all.21.came_ref = bf16[32,2,16,128]{3,2,1,0:T(8,128)(2,1)S(1)} all-to-all(bf16[32,2,16,128]{3,2,1,0:T(8,128)(2,1)S(1)} %bitcast.12), channel_id=1, replica_groups=mesh['far'=2,'x'=2,'y'=4,'c'=2,'z'=4] {'x','y','z'}, dimensions={0} | all-to-all | bytes 524288 | tf_op jit(solution)/shard_map/all_to_all | solution.py:326
  35.9 0.1 shard_map.105
  36.0 0.0 slice-start.4
  36.0 17.8 %all_to_all.22.whole_ref = bf16[64,2,16,128]{3,2,1,0:T(8,128)(2,1)S(1)} all-to-all(bf16[64,2,16,128]{3,2,1,0:T(8,128)(2,1)S(1)} %shard_map.105), channel_id=1, replica_groups=mesh['far'=2,'x'=2,'y'=4,'c'=2,'z'=4] {'far','x','y','z'}, dimensions={0} | all-to-all | bytes 1048576 | tf_op jit(solution)/shard_map/all_to_all | solution.py:326
  53.9 0.0 collective-permute-start.1
  53.9 0.0 copy-done.1
  53.9 0.0 slice-done
  53.9 0.0 slice-done.2
  53.9 0.0 slice-done.1
  53.9 0.0 slice-done.3
  53.9 0.0 slice-start.5
  54.0 1.9 %shard_map.106 = (f32[208,16]{1,0:T(8,128)S(1)}, f32[208,16]{1,0:T(8,128)S(1)}, f32[16,128]{1,0:T(8,128)S(1)}, f32[16,128]{1,0:T(8,128)S(1)}) custom-call(bf16[64,2,16,128]{3,2,1,0:T(8,128)(2,1)S(1)} %all_to_all.22.whole_ref, f32[128,128]{1,0:T(8,128)S(1)} %bitcast_convert_fusion.gain_ref, bf16[208,16384]{1,0:T(8,128)(2,1)S(1)} %bitcast.7, ...), custom_call_target="tpu_custom_call" | custom-call | flops 1000000000 | bytes 1048576 | tf_op jit(solution)/shard_map/pallas_call | solution.py:29
  55.9 0.0 collective-permute-done.1.whole_ref
  55.9 2.5 %shard_map.107 = (bf16[64,16,128]{2,1,0:T(8,128)(2,1)S(1)}, bf16[16,208]{1,0:T(8,128)(2,1)S(1)}) custom-call(bf16[64,2,16,128]{3,2,1,0:T(8,128)(2,1)S(1)} %collective-permute-done.1.whole_ref, f32[128,128]{1,0:T(8,128)S(1)} %bitcast_convert_fusion.gain_ref, bf16[208,16384]{1,0:T(8,128)(2,1)S(1)} %bitcast.7, bf16[208,16384]{1,0:T(8,128)(2,1)S(1)} %bitcast.9, ...), custom_call_target="tpu_custom_call" | custom-call | bytes 1048576 | tf_op jit(solution)/shard_map/pallas_call | solution.py:29
  58.4 0.6 collective-permute-start.2
  59.0 0.5 shard_map.108.own_ref
  59.5 0.6 collective-permute-done.2.came_ref
  60.2 15.7 %all_to_all.23.came_ref = bf16[64,16,128]{2,1,0:T(8,128)(2,1)S(1)} all-to-all(bf16[64,16,128]{2,1,0:T(8,128)(2,1)S(1)} %shard_map.109), channel_id=1, replica_groups=mesh['far'=2,'x'=2,'y'=4,'c'=2,'z'=4] {'far','x','y','z'}, dimensions={0} | all-to-all | bytes 524288 | tf_op jit(solution)/shard_map/all_to_all | solution.py:326
  75.8 0.7 shard_map.110
  (9 shorter events, 0.1 us)
Async XLA Ops:
  1.7 16.1 %copy-start = (bf16[128,16384]{1,0:T(8,128)(2,1)S(1)}, bf16[128,16384]{1,0:T(8,128)(2,1)}, u32[]{:S(2)}) copy-start(bf16[128,16384]{1,0:T(8,128)(2,1)} %weight_ref.4) | copy-start | bytes 12582916
  2.0 51.9 %slice-start = ((s8[6815744]{0:T(1024)(128)(4,1)}), s8[4194304]{0:T(1024)(128)(4,1)S(1)}, s32[]{:S(2)}) async-start(s8[6815744]{0:T(1024)(128)(4,1)} %bitcast.6), calls=%async_computation.4 | async-start | bytes 8388608
  2.0 51.9 %slice-start.2 = ((s8[6815744]{0:T(1024)(128)(4,1)}), s8[4194304]{0:T(1024)(128)(4,1)S(1)}, s32[]{:S(2)}) async-start(s8[6815744]{0:T(1024)(128)(4,1)} %bitcast.8), calls=%async_computation.6 | async-start | bytes 8388608
  17.9 36.0 %slice-start.1 = ((s8[6815744]{0:T(1024)(128)(4,1)}), s8[2621440]{0:T(1024)(128)(4,1)S(1)}, s32[]{:S(2)}) async-start(s8[6815744]{0:T(1024)(128)(4,1)} %bitcast.6), calls=%async_computation.5 | async-start | bytes 5242880
  17.9 36.0 %slice-start.3 = ((s8[6815744]{0:T(1024)(128)(4,1)}), s8[2621440]{0:T(1024)(128)(4,1)S(1)}, s32[]{:S(2)}) async-start(s8[6815744]{0:T(1024)(128)(4,1)} %bitcast.8), calls=%async_computation.7 | async-start | bytes 5242880
  18.5 35.4 %copy-start.1 = (bf16[16384]{0:T(1024)(128)(2,1)S(1)}, bf16[16384]{0:T(1024)(128)(2,1)}, u32[]{:S(2)}) copy-start(bf16[16384]{0:T(1024)(128)(2,1)} %param.16) | copy-start | bytes 98308
  18.5 1.6 %collective-permute-start = (bf16[64,16,128]{2,1,0:T(8,128)(2,1)S(1)}, bf16[64,16,128]{2,1,0:T(8,128)(2,1)S(1)}, u32[]{:S(2)}, u32[]{:S(2)}) collective-permute-start(bf16[64,16,128]{2,1,0:T(8,128)(2,1)S(1)} %get-tuple-element.21), channel_id=1, source_target_pairs={{0,4},{4,0},{1,5},{5,1},{2,6},{6,2},{3,7},{7,3},{8,12},{12,8},{9,1... | collective-permute-start | bytes 786440 | tf_op jit(solution)/shard_map/ppermute | solution.py:330
  36.0 19.9 %slice-start.4 = ((s8[6815744]{0:T(1024)(128)(4,1)}), s8[4194304]{0:T(1024)(128)(4,1)S(1)}, s32[]{:S(2)}) async-start(s8[6815744]{0:T(1024)(128)(4,1)} %bitcast.10), calls=%async_computation.8 | async-start | bytes 8388608
  53.9 2.0 %collective-permute-start.1 = (bf16[64,2,16,128]{3,2,1,0:T(8,128)(2,1)S(1)}, bf16[64,2,16,128]{3,2,1,0:T(8,128)(2,1)S(1)}, u32[]{:S(2)}, u32[]{:S(2)}) collective-permute-start(bf16[64,2,16,128]{3,2,1,0:T(8,128)(2,1)S(1)} %all_to_all.22.whole_ref), channel_id=1, source_target_pairs={{0,4},{4,0},{1,5},{5,1},{2,6},{6,2},{3,7},{7,3},{8,12},{12,8},{9,1... | collective-permute-start | bytes 1572872 | tf_op jit(solution)/shard_map/ppermute | solution.py:330
  53.9 2.0 %slice-start.5 = ((s8[6815744]{0:T(1024)(128)(4,1)}), s8[2621440]{0:T(1024)(128)(4,1)S(1)}, s32[]{:S(2)}) async-start(s8[6815744]{0:T(1024)(128)(4,1)} %bitcast.10), calls=%async_computation.9 | async-start | bytes 5242880
  58.4 1.7 %collective-permute-start.2 = (bf16[64,16,128]{2,1,0:T(8,128)(2,1)S(1)}, bf16[64,16,128]{2,1,0:T(8,128)(2,1)S(1)}, u32[]{:S(2)}, u32[]{:S(2)}) collective-permute-start(bf16[64,16,128]{2,1,0:T(8,128)(2,1)S(1)} %get-tuple-element.28), channel_id=1, source_target_pairs={{0,4},{4,0},{1,5},{5,1},{2,6},{6,2},{3,7},{7,3},{8,12},{12,8},{9,1... | collective-permute-start | bytes 786440 | tf_op jit(solution)/shard_map/ppermute | solution.py:330

commit v6 on v5

--- a/solution.py
+++ b/solution.py
@@ -7,8 +7,9 @@
 from jax.experimental.pallas import tpu as pltpu
 from jax.sharding import Mesh, PartitionSpec as P
 
-KV = ("far", "x", "y", "c")
-ALL = ("far", "x", "y", "c", "z")
+KV = ("x", "far", "y", "c")
+ALL = ("x", "far", "y", "c", "z")
+PLACES = ("x", "far", "y", "z")
 CHIPS = ("far", "x", "y", "z")
 NEAR = ("x", "y", "z")
 LANES = 128
@@ -57,8 +58,8 @@
     slots = k_ref.shape[1]
     span = slots // groups
     size = heads // groups
-    near = flat_index(("x", "y", "c", "z"))
-    distance = lax.axis_size(("x", "y", "c", "z"))
+    distance = lax.axis_size(("y", "c", "z"))
+    near = flat_index(ALL) - lax.axis_index("far") * distance
     starts = [pl.multiple_of((near + i * distance) * LANES, LANES) for i in range(lax.axis_size("far"))]
     loads = [
         pltpu.make_async_copy(source, target, sems.at[i])
@@ -163,6 +164,13 @@
     return 1 - lax.axis_index("c")
 
 
+def half_and_near(piece):
+    size = lax.axis_size("y")
+    row, inside = divmod(piece, size * lax.axis_size("far"))
+    half, y = divmod(inside, size)
+    return half, row * size + y
+
+
 def half_product(left, weight_ref, side, out_ref, paired):
     per = lax.axis_size("z")
     run = per * LANES
@@ -170,7 +178,7 @@
     halves = lax.axis_size("far")
     for piece in range(places):
         product = jnp.dot(left, weight_ref[:, columns_of(piece, side, run)], preferred_element_type=jnp.float32)
-        half, near = divmod(piece, places // halves)
+        half, near = half_and_near(piece)
         for j in range(per):
             at = (near * per + j) * halves + half if paired else piece * per + j
             out_ref[at] = product[:, j * LANES : (j + 1) * LANES].astype(out_ref.dtype)
@@ -253,9 +261,8 @@
 def gate_up(side, whole_ref, gain_ref, gate_ref, up_ref, gate, up, square):
     per = lax.axis_size("z")
     run = per * LANES
-    places = whole_ref.shape[0] // per
-    for piece in range(places):
-        half, near = divmod(piece, places // lax.axis_size("far"))
+    for piece in range(whole_ref.shape[0] // per):
+        half, near = half_and_near(piece)
         parts = []
         for j in range(per):
             part = stream_block(whole_ref, near * per + j, half)
@@ -345,11 +352,11 @@
     *sums, stream = first_half(whole, gain, gate_weight, up_weight)
     sent, hidden = second_half(other(whole), gain, gate_weight, up_weight, down_weight, sums)
     partial = add(own_half(hidden, down_weight, False), other(sent))
-    return final_sum(stream, swap(partial, CHIPS))
+    return final_sum(stream, swap(partial, PLACES))
 
 
 def solution(mesh):
-    fine = Mesh(mesh.devices.reshape(2, 2, 4, 2, 4), ALL)
+    fine = Mesh(mesh.devices.reshape(4, 2, 2, 2, 4), ALL)
     placed = (
         P(None, "z", None),
         P(None, KV, "z", None),

time: 76.7 us -> 76.5 us (level)
  no operation moved by 1% of the time
where the time goes in v6:
time: 76.5 us; the launch traced here: 76.3 us
  blocking collectives  64.8 us (85%)
  Pallas kernels  8.78 us (11%)
  waiting for transfers between devices  1.52 us (2%)
  starting transfers between devices  0.9 us (1%)
    all_to_all x4, blocking collectives, swap(): return lax.all_to_all(blocks, axes, split_axis=0, concat_axis=0, tiled=True)  64.8 us
    pallas_call x11, Pallas kernels, call(): pl.pallas_call(kernel, out_shape=shapes, in_specs=[pl.BlockSpec(memory_sp...  8.78 us
  transfers between devices with their start and end apart: 3, of which 2 were waited for; matrix products, arithmetic and copies ran while one was open for 0% of the time, Pallas kernels for 4%

profile of v6, /device:TPU:0, one launch (start us, length us, event | category | flops | bytes accessed | tf_op | source)
XLA Modules:
  0.0 76.3 jit_solution(11344697730869003101)
XLA Ops:
  0.0 1.7 %shard_map.100 = (bf16[16,32,128]{2,1,0:T(8,128)(2,1)S(1)}, f32[16,32,128]{2,1,0:T(8,128)S(1)}, bf16[16,128,128]{2,1,0:T(8,128)(2,1)S(1)}, bf16[2,16,128]{2,1,0:T(8,128)(2,1)S(1)}) custom-call(s32[16]{0:T(128)} %lengths_hbm.1, bf16[16,32,128]{2,1,0:T(8,128)(2,1)} %q_hbm.1, bf16[16,128,128]{2,1,0:T(8,128)(2,1)} %bitcast.13, bf16[16,128,128]{2,1,0:T(8,128)(2,1)} %bitcast.14, ...), custom_call_target="tpu_custom_call" | custom-call | bytes 1048576 | tf_op jit(solution)/shard_map/pallas_call | solution.py:30
  1.7 0.0 copy-start
  1.8 0.3 shard_map.101
  2.0 0.0 slice-start
  2.0 0.0 slice-start.2
  2.1 15.8 %all_to_all.20.came_ref = bf16[32,24,128]{2,1,0:T(8,128)(2,1)S(1)} all-to-all(bf16[32,24,128]{2,1,0:T(8,128)(2,1)S(1)} %shard_map.101), channel_id=1, replica_groups=mesh['x'=4,'far'=2,'y'=2,'c'=2,'z'=4] {'x','far','y','c'}, dimensions={0} | all-to-all | bytes 393216 | tf_op jit(solution)/shard_map/all_to_all | solution.py:333
  17.9 0.0 copy-done
  17.9 0.6 shard_map.102
  18.5 0.0 copy-start.1
  18.5 0.3 collective-permute-start
  18.8 0.4 shard_map.103.own_ref
  19.2 0.9 %collective-permute-done.came_ref = bf16[64,16,128]{2,1,0:T(8,128)(2,1)S(1)} collective-permute-done((bf16[64,16,128]{2,1,0:T(8,128)(2,1)S(1)}, bf16[64,16,128]{2,1,0:T(8,128)(2,1)S(1)}, u32[]{:S(2)}, u32[]{:S(2)}) %collective-permute-start) | collective-permute-done | bytes 262176 | tf_op jit(solution)/shard_map/ppermute | solution.py:337
  20.1 0.1 shard_map.104
  20.2 15.9 %all_to_all.21.came_ref = bf16[32,2,16,128]{3,2,1,0:T(8,128)(2,1)S(1)} all-to-all(bf16[32,2,16,128]{3,2,1,0:T(8,128)(2,1)S(1)} %bitcast.12), channel_id=1, replica_groups=mesh['x'=4,'far'=2,'y'=2,'c'=2,'z'=4] {'x','y','z'}, dimensions={0} | all-to-all | bytes 524288 | tf_op jit(solution)/shard_map/all_to_all | solution.py:333
  36.1 0.1 shard_map.105
  36.1 0.0 slice-start.4
  36.1 17.6 %all_to_all.22.whole_ref = bf16[64,2,16,128]{3,2,1,0:T(8,128)(2,1)S(1)} all-to-all(bf16[64,2,16,128]{3,2,1,0:T(8,128)(2,1)S(1)} %shard_map.105), channel_id=1, replica_groups=mesh['x'=4,'far'=2,'y'=2,'c'=2,'z'=4] {'far','x','y','z'}, dimensions={0} | all-to-all | bytes 1048576 | tf_op jit(solution)/shard_map/all_to_all | solution.py:333
  53.8 0.0 collective-permute-start.1
  53.8 0.0 copy-done.1
  53.8 0.0 slice-done
  53.8 0.0 slice-done.2
  53.8 0.0 slice-done.1
  53.8 0.0 slice-done.3
  53.9 0.0 slice-start.5
  53.9 1.9 %shard_map.106 = (f32[208,16]{1,0:T(8,128)S(1)}, f32[208,16]{1,0:T(8,128)S(1)}, f32[16,128]{1,0:T(8,128)S(1)}, f32[16,128]{1,0:T(8,128)S(1)}) custom-call(bf16[64,2,16,128]{3,2,1,0:T(8,128)(2,1)S(1)} %all_to_all.22.whole_ref, f32[128,128]{1,0:T(8,128)S(1)} %bitcast_convert_fusion.gain_ref, bf16[208,16384]{1,0:T(8,128)(2,1)S(1)} %bitcast.7, ...), custom_call_target="tpu_custom_call" | custom-call | flops 1000000000 | bytes 1048576 | tf_op jit(solution)/shard_map/pallas_call | solution.py:30
  55.8 0.0 collective-permute-done.1.whole_ref
  55.8 2.5 %shard_map.107 = (bf16[64,16,128]{2,1,0:T(8,128)(2,1)S(1)}, bf16[16,208]{1,0:T(8,128)(2,1)S(1)}) custom-call(bf16[64,2,16,128]{3,2,1,0:T(8,128)(2,1)S(1)} %collective-permute-done.1.whole_ref, f32[128,128]{1,0:T(8,128)S(1)} %bitcast_convert_fusion.gain_ref, bf16[208,16384]{1,0:T(8,128)(2,1)S(1)} %bitcast.7, bf16[208,16384]{1,0:T(8,128)(2,1)S(1)} %bitcast.9, ...), custom_call_target="tpu_custom_call" | custom-call | bytes 1048576 | tf_op jit(solution)/shard_map/pallas_call | solution.py:30
  58.3 0.6 collective-permute-start.2
  58.9 0.5 shard_map.108.own_ref
  59.4 0.6 collective-permute-done.2.came_ref
  60.1 15.5 %all_to_all.23.came_ref = bf16[64,16,128]{2,1,0:T(8,128)(2,1)S(1)} all-to-all(bf16[64,16,128]{2,1,0:T(8,128)(2,1)S(1)} %shard_map.109), channel_id=1, replica_groups=mesh['x'=4,'far'=2,'y'=2,'c'=2,'z'=4] {'x','far','y','z'}, dimensions={0} | all-to-all | bytes 524288 | tf_op jit(solution)/shard_map/all_to_all | solution.py:333
  75.6 0.7 shard_map.110
  (9 shorter events, 0.1 us)
Async XLA Ops:
  1.7 16.1 %copy-start = (bf16[128,16384]{1,0:T(8,128)(2,1)S(1)}, bf16[128,16384]{1,0:T(8,128)(2,1)}, u32[]{:S(2)}) copy-start(bf16[128,16384]{1,0:T(8,128)(2,1)} %weight_ref.4) | copy-start | bytes 12582916
  2.0 51.8 %slice-start = ((s8[6815744]{0:T(1024)(128)(4,1)}), s8[4194304]{0:T(1024)(128)(4,1)S(1)}, s32[]{:S(2)}) async-start(s8[6815744]{0:T(1024)(128)(4,1)} %bitcast.6), calls=%async_computation.4 | async-start | bytes 8388608
  2.0 51.8 %slice-start.2 = ((s8[6815744]{0:T(1024)(128)(4,1)}), s8[4194304]{0:T(1024)(128)(4,1)S(1)}, s32[]{:S(2)}) async-start(s8[6815744]{0:T(1024)(128)(4,1)} %bitcast.8), calls=%async_computation.6 | async-start | bytes 8388608
  17.9 36.0 %slice-start.1 = ((s8[6815744]{0:T(1024)(128)(4,1)}), s8[2621440]{0:T(1024)(128)(4,1)S(1)}, s32[]{:S(2)}) async-start(s8[6815744]{0:T(1024)(128)(4,1)} %bitcast.6), calls=%async_computation.5 | async-start | bytes 5242880
  17.9 36.0 %slice-start.3 = ((s8[6815744]{0:T(1024)(128)(4,1)}), s8[2621440]{0:T(1024)(128)(4,1)S(1)}, s32[]{:S(2)}) async-start(s8[6815744]{0:T(1024)(128)(4,1)} %bitcast.8), calls=%async_computation.7 | async-start | bytes 5242880
  18.5 35.3 %copy-start.1 = (bf16[16384]{0:T(1024)(128)(2,1)S(1)}, bf16[16384]{0:T(1024)(128)(2,1)}, u32[]{:S(2)}) copy-start(bf16[16384]{0:T(1024)(128)(2,1)} %param.16) | copy-start | bytes 98308
  18.5 1.6 %collective-permute-start = (bf16[64,16,128]{2,1,0:T(8,128)(2,1)S(1)}, bf16[64,16,128]{2,1,0:T(8,128)(2,1)S(1)}, u32[]{:S(2)}, u32[]{:S(2)}) collective-permute-start(bf16[64,16,128]{2,1,0:T(8,128)(2,1)S(1)} %get-tuple-element.21), channel_id=1, source_target_pairs={{0,4},{4,0},{1,5},{5,1},{2,6},{6,2},{3,7},{7,3},{8,12},{12,8},{9,1... | collective-permute-start | bytes 786440 | tf_op jit(solution)/shard_map/ppermute | solution.py:337
  36.1 19.7 %slice-start.4 = ((s8[6815744]{0:T(1024)(128)(4,1)}), s8[4194304]{0:T(1024)(128)(4,1)S(1)}, s32[]{:S(2)}) async-start(s8[6815744]{0:T(1024)(128)(4,1)} %bitcast.10), calls=%async_computation.8 | async-start | bytes 8388608
  53.8 2.0 %collective-permute-start.1 = (bf16[64,2,16,128]{3,2,1,0:T(8,128)(2,1)S(1)}, bf16[64,2,16,128]{3,2,1,0:T(8,128)(2,1)S(1)}, u32[]{:S(2)}, u32[]{:S(2)}) collective-permute-start(bf16[64,2,16,128]{3,2,1,0:T(8,128)(2,1)S(1)} %all_to_all.22.whole_ref), channel_id=1, source_target_pairs={{0,4},{4,0},{1,5},{5,1},{2,6},{6,2},{3,7},{7,3},{8,12},{12,8},{9,1... | collective-permute-start | bytes 1572872 | tf_op jit(solution)/shard_map/ppermute | solution.py:337
  53.9 2.0 %slice-start.5 = ((s8[6815744]{0:T(1024)(128)(4,1)}), s8[2621440]{0:T(1024)(128)(4,1)S(1)}, s32[]{:S(2)}) async-start(s8[6815744]{0:T(1024)(128)(4,1)} %bitcast.10), calls=%async_computation.9 | async-start | bytes 5242880
  58.3 1.7 %collective-permute-start.2 = (bf16[64,16,128]{2,1,0:T(8,128)(2,1)S(1)}, bf16[64,16,128]{2,1,0:T(8,128)(2,1)S(1)}, u32[]{:S(2)}, u32[]{:S(2)}) collective-permute-start(bf16[64,16,128]{2,1,0:T(8,128)(2,1)S(1)} %get-tuple-element.28), channel_id=1, source_target_pairs={{0,4},{4,0},{1,5},{5,1},{2,6},{6,2},{3,7},{7,3},{8,12},{12,8},{9,1... | collective-permute-start | bytes 786440 | tf_op jit(solution)/shard_map/ppermute | solution.py:337
